TPU v7x, 32 devices: a whole 2x2x4 slice. The times are simulated.
32 devices in a mesh: groups: 2 (over y), emit: 4 (over z), recv: 4 (over x, core).
Axes of the slice: x: 2, y: 2, z: 4, core: 2. Of those that a mesh axis runs over, the one named last changes fastest.
Arguments:
- positions: float32 [3, 8192], P(None, ('groups', 'emit', 'recv')), parts along dimension 1, may hold values from 0 to 1
- angles: float32 [2, 8192], P(None, ('groups', 'emit', 'recv')), parts along dimension 1, may hold values from -3.140625 to 3.140625
- areas: float32 [8192], P(('groups', 'emit', 'recv')), parts along dimension 0, may hold values from 0.00024414062 to 0.00390625
- emissivity: float32 [8192], P(('groups', 'emit', 'recv')), parts along dimension 0, may hold values from 0.1 to 0.9
- emission: float32 [32, 8192], P(None, ('groups', 'emit', 'recv')), parts along dimension 1, may hold values from 0.5 to 2
- radiosity_in: float32 [32, 8192], P(None, ('groups', 'emit', 'recv')), parts along dimension 1, may hold values from 0.2 to 2
- adjoint_in: float32 [32, 8192], P(None, ('groups', 'emit', 'recv')), parts along dimension 1, may hold values from 0 to 1.5
- visibility: int32 [64, 32], P(('groups', 'emit')), parts along dimension 0, may hold values 0 or 1
- inlet_patches: int32 [4096], P('groups'), parts along dimension 0, may hold values from 0 to 4095
- inlet_weights: float32 [32, 4096], P(None, 'groups'), parts along dimension 1, may hold values from 0.5 to 2
Outputs:
- radiosity_out: float32 [32, 8192], P(None, ('groups', 'emit', 'recv')), parts along dimension 1
- adjoint_out: float32 [32, 8192], P(None, ('groups', 'emit', 'recv')), parts along dimension 1
- emissivity_grad: float32 [8192], P(('groups', 'emit', 'recv')), parts along dimension 0
There are 2 independent parts, one for each index of `groups`. A program takes and returns all parts, laid end to end along the dimension named above; each array names one. Nothing has to cross between parts.
Inputs may be any that keep to these rules, and one draw needn't show every extreme that they name: `inlet_patches`: an inlet patch may be listed more than once.
All inputs are finite; a program needn't handle non-finite values. No bound on the sum of `visibility` on one device may be relied on, other than what follows from the above.
Results may differ from a plain program's by a relative error of at most 0.0003.
Values may be sent and summed in bfloat16 or wider, within the bound.
A program may use at most 64 MiB of HBM per device.

v0:
```python
import math

import jax
import jax.numpy as jnp
from jax import lax
from jax.sharding import PartitionSpec as P

BLK = 128


def patch_geometry(positions, angles, areas):
    polar = angles[0]
    azimuth = angles[1]
    normal = jnp.stack(
        [jnp.sin(polar) * jnp.cos(azimuth), jnp.sin(polar) * jnp.sin(azimuth), jnp.cos(polar)]
    )
    return jnp.concatenate([positions, normal, areas[None, :]], axis=0)


def view_tile(row_geom, col_geom, block_mask):
    delta_x = col_geom[0][None, :] - row_geom[0][:, None]
    delta_y = col_geom[1][None, :] - row_geom[1][:, None]
    delta_z = col_geom[2][None, :] - row_geom[2][:, None]
    dist_sq = delta_x * delta_x + delta_y * delta_y + delta_z * delta_z
    cos_emit = jnp.maximum(
        row_geom[3][:, None] * delta_x
        + row_geom[4][:, None] * delta_y
        + row_geom[5][:, None] * delta_z,
        0.0,
    )
    cos_recv = jnp.maximum(
        -(
            col_geom[3][None, :] * delta_x
            + col_geom[4][None, :] * delta_y
            + col_geom[5][None, :] * delta_z
        ),
        0.0,
    )
    patch_area = row_geom[6][:, None]
    spread = dist_sq + patch_area
    kernel = cos_emit * cos_recv * patch_area / (math.pi * spread * spread)
    row_blocks, col_blocks = block_mask.shape
    rows_total = row_geom.shape[1]
    cols_total = col_geom.shape[1]
    expanded = jnp.broadcast_to(
        block_mask[:, None, :, None],
        (row_blocks, rows_total // row_blocks, col_blocks, cols_total // col_blocks),
    ).reshape(rows_total, cols_total)
    return (expanded * kernel).astype(jnp.bfloat16)


def block_width():
    return 128


def local(
    positions,
    angles,
    areas,
    emissivity,
    emission,
    radiosity_in,
    adjoint_in,
    visibility,
    inlet_patches,
    inlet_weights,
):
    emit_count = lax.axis_size("emit")
    recv_count = lax.axis_size("recv")
    emit_index = lax.axis_index("emit")
    recv_index = lax.axis_index("recv")
    own_count = areas.shape[0]
    cases = emission.shape[0]
    geometry = patch_geometry(positions, angles, areas)
    reflect = 1.0 - emissivity
    own_weights = (reflect[None, :] * adjoint_in).astype(jnp.bfloat16)
    own_values = radiosity_in.astype(jnp.bfloat16)
    mask_rows = visibility.shape[0]
    per_block = visibility.shape[1] // emit_count
    own_blocks = own_count // BLK
    folded_mask = visibility.astype(jnp.float32).reshape(mask_rows, emit_count, per_block)
    tile_mask = lax.dynamic_slice_in_dim(
        folded_mask, recv_index * own_blocks, own_blocks, 2
    ).reshape(mask_rows, emit_count * own_blocks)
    row_total = own_count * recv_count
    col_total = own_count * emit_count
    row_values = lax.all_gather(own_values, "recv", axis=1, tiled=True)
    col_weight = lax.all_gather(own_weights, "emit", axis=1, tiled=True)
    start_state = (
        jnp.zeros((cases, col_total), jnp.float32),
        jnp.zeros((cases, row_total), jnp.float32),
    )
    col_geom = lax.all_gather(geometry, "emit", axis=1, tiled=True)
    geom_piece = lax.all_gather(geometry, "recv", axis=1, tiled=True)
    count = geom_piece.shape[1]
    width = block_width()

    def inner(number, state):
        fwd_total, adj_total = state
        offset = number * width
        geom_part = lax.dynamic_slice_in_dim(geom_piece, offset, width, 1)
        value_part = lax.dynamic_slice_in_dim(row_values, offset, width, 1)
        mask_part = lax.dynamic_slice_in_dim(tile_mask, offset // BLK, width // BLK, 0)
        tile = view_tile(geom_part, col_geom, mask_part)
        fwd_total = fwd_total + jnp.dot(value_part, tile, preferred_element_type=jnp.float32)
        adj_part = lax.dot_general(
            col_weight, tile, (((1,), (1,)), ((), ())), preferred_element_type=jnp.float32
        )
        adj_total = lax.dynamic_update_slice_in_dim(adj_total, adj_part, offset, 1)
        return (fwd_total, adj_total)

    forward, adjoint = lax.fori_loop(0, count // width, inner, start_state)
    incoming = lax.psum_scatter(forward, "emit", scatter_dimension=1, tiled=True)
    returned = lax.psum_scatter(adjoint, "recv", scatter_dimension=1, tiled=True)
    own_ids = (emit_index * recv_count + recv_index) * own_count + lax.iota(jnp.int32, own_count)
    selector = (inlet_patches[:, None] == own_ids[None, :]).astype(jnp.float32)
    source = jnp.dot(
        inlet_weights, selector, precision=lax.Precision.HIGHEST, preferred_element_type=jnp.float32
    )
    radiosity_out = emissivity[None, :] * emission + reflect[None, :] * incoming
    adjoint_out = source + returned
    emissivity_grad = jnp.sum(adjoint_out * (emission - incoming), axis=0)
    return (radiosity_out, adjoint_out, emissivity_grad)


def solution(mesh):
    placed = (
        P(None, ("groups", "emit", "recv")),
        P(None, ("groups", "emit", "recv")),
        P(("groups", "emit", "recv")),
        P(("groups", "emit", "recv")),
        P(None, ("groups", "emit", "recv")),
        P(None, ("groups", "emit", "recv")),
        P(None, ("groups", "emit", "recv")),
        P(("groups", "emit"), None),
        P("groups"),
        P(None, "groups"),
    )
    return jax.shard_map(
        local,
        mesh=mesh,
        in_specs=placed,
        out_specs=(
            P(None, ("groups", "emit", "recv")),
            P(None, ("groups", "emit", "recv")),
            P(("groups", "emit", "recv")),
        ),
        check_vma=False,
    )
```

profile of v0, /device:TPU:0, one launch (start us, length us, event | category | flops | bytes accessed | tf_op | source)
XLA Modules:
  0.0 115.8 jit_solution(4974398801967030085)
XLA Ops:
  7.2 0.8 slice_cosine_fusion
  8.8 14.8 %all_gather.14 = f32[7,1024]{1,0:T(8,128)S(1)} all-gather(f32[7,256]{1,0:T(8,128)S(1)} %concatenate.3), channel_id=1, replica_groups=mesh['groups'=2,'emit'=4,'recv'=4] {'emit'}, dimensions={1}, use_global_device_ids=true | all-gather | bytes 35840 | tf_op jit(solution)/shard_map/all_gather | solution.py:93
  23.6 5.2 %all_gather.13 = f32[7,1024]{1,0:T(8,128)S(1)} all-gather(f32[7,256]{1,0:T(8,128)S(1)} %concatenate.3), channel_id=1, replica_groups=mesh['groups'=2,'emit'=4,'recv'=4] {'recv'}, dimensions={1}, use_global_device_ids=true | all-gather | bytes 35840 | tf_op jit(solution)/shard_map/all_gather | solution.py:94
  31.1 5.2 %all_gather.12 = bf16[32,1024]{1,0:T(8,128)(2,1)S(1)} all-gather(bf16[32,256]{1,0:T(8,128)(2,1)S(1)} %convert_element_type.20), channel_id=1, replica_groups=mesh['groups'=2,'emit'=4,'recv'=4] {'recv'}, dimensions={1}, use_global_device_ids=true | all-gather | bytes 81920 | tf_op jit(solution)/shard_map/all_gather | solution.py:87
  36.3 13.1 %all_gather.15 = bf16[32,1024]{1,0:T(8,128)(2,1)S(1)} all-gather(bf16[32,256]{1,0:T(8,128)(2,1)S(1)} %multiply_convert_fusion), channel_id=1, replica_groups=mesh['groups'=2,'emit'=4,'recv'=4] {'emit'}, dimensions={1}, use_global_device_ids=true | all-gather | bytes 81920 | tf_op jit(solution)/shard_map/all_gather | solution.py:88
  49.4 13.7 %while.18 = (s32[]{:T(128)}, f32[32,1024]{1,0:T(8,128)S(1)}, f32[32,1024]{1,0:T(8,128)S(1)}, bf16[32,1024]{1,0:T(8,128)(2,1)S(1)}, f32[8,8]{1,0:T(8,128)S(1)}, /...) while((s32[]{:T(128)}, f32[32,1024]{1,0:T(8,128)S(1)}, ...), condition=%wide.region_1.2_spmd.clone, body=%wide.region_0.1_spmd.clone.sunk | while | flops 24444952 | bytes 484852 | solution.py:112
  49.6 0.8 convolution_add_fusion.2
  50.4 0.8 fusion.47
  51.3 0.8 convolution_add_fusion.2
  53.0 0.8 convolution_add_fusion.2
  53.8 0.8 fusion.47
  54.7 0.8 convolution_add_fusion.2
  55.5 0.8 fusion.47
  56.4 0.8 convolution_add_fusion.2
  57.2 0.8 fusion.47
  58.1 0.8 convolution_add_fusion.2
  58.9 0.8 fusion.47
  59.8 0.8 convolution_add_fusion.2
  60.6 0.8 fusion.47
  61.5 0.8 convolution_add_fusion.2
  62.4 0.8 fusion.47
  64.6 20.0 %reduce-scatter.5.cloned.1.call-done = f32[32,256]{1,0:T(8,128)} async-done(((f32[32,1024]{1,0:T(8,128)}), f32[32,256]{1,0:T(8,128)}) %reduce-scatter.5.cloned.1.call-update) | async-done | bytes 32784 | tf_op jit(solution)/shard_map/reduce_scatter | solution.py:114
  84.6 21.6 %reduce-scatter.3.cloned.1.call-done = f32[32,256]{1,0:T(8,128)} async-done(((f32[32,1024]{1,0:T(8,128)}), f32[32,256]{1,0:T(8,128)}) %reduce-scatter.3.cloned.1.call-update) | async-done | bytes 32784 | tf_op jit(solution)/shard_map/reduce_scatter | solution.py:113
  106.2 2.8 %multiply_reduce_fusion = (f32[256]{0:T(256)}, f32[32,256]{1,0:T(8,128)}, f32[32,256]{1,0:T(8,128)}) fusion(f32[32,256]{1,0:T(8,128)S(1)} %copy-done.5, f32[32,256]{1,0:T(8,128)} %reduce-scatter.3.cloned.1.call-done, f32[256]{0:T(256)S(1)} %broadcast_subtract_fusion, f32[256]{0:T(256)S(1)} %copy-done.4, f32[32,256]{1,0:T(8,128)} %reduce-scatter.5.cloned.1.call-done, ...), kind=kOutput, calls=%fused_computation.47 | convolution fusion | flops 201907968 | bytes 438272 | tf_op jit(solution)/shard_map/dot_general | solution.py:117
  (70 shorter events, 6.1 us)
Async XLA Ops:
  7.2 99.0 %copy-start = (f32[32,2048]{1,0:T(8,128)S(1)}, f32[32,2048]{1,0:T(8,128)}, u32[]{:S(2)}) copy-start(f32[32,2048]{1,0:T(8,128)} %param.21) | copy-start | bytes 786436
  7.2 29.1 %copy-start.3 = (f32[32,256]{1,0:T(8,128)S(1)}, f32[32,256]{1,0:T(8,128)}, u32[]{:S(2)}) copy-start(f32[32,256]{1,0:T(8,128)} %param.18) | copy-start | bytes 98308
  7.2 77.4 %reduce-scatter.5.cloned.1.call-start = ((), (), s32[]{:S(2)}) async-start(), calls=%async_computation.3 | async-start | bytes 163840 | tf_op jit(solution)/shard_map/reduce_scatter | solution.py:114
  63.1 0.7 copy-start.1
  63.1 0.7 copy-start.2
  63.1 43.0 %copy-start.4 = (f32[256]{0:T(256)S(1)}, f32[256]{0:T(256)}, u32[]{:S(2)}) copy-start(f32[256]{0:T(256)} %param.15) | copy-start | bytes 3076
  63.2 43.0 %copy-start.5 = (f32[32,256]{1,0:T(8,128)S(1)}, f32[32,256]{1,0:T(8,128)}, u32[]{:S(2)}) copy-start(f32[32,256]{1,0:T(8,128)} %param.16) | copy-start | bytes 98308
  63.2 43.0 %copy-start.6 = (s32[2048]{0:T(1024)S(1)}, s32[2048]{0:T(1024)}, u32[]{:S(2)}) copy-start(s32[2048]{0:T(1024)} %param.20) | copy-start | bytes 24580
  63.8 42.3 %reduce-scatter.3.cloned.1.call-start = ((), (), s32[]{:S(2)}) async-start(), calls=%async_computation.2 | async-start | bytes 163840 | tf_op jit(solution)/shard_map/reduce_scatter | solution.py:113
Sparse Core Ops, SparseCore 0:
  63.9 20.5 reduce-scatter.4
  86.9 19.1 reduce-scatter.2
where the time goes:
time: 116 us
  waiting for transfers between devices  42.3 us (36%)
  blocking collectives  38.3 us (33%)
  matrix products  15.3 us (13%)
  between operations  14.1 us (12%)
  other arithmetic  2.97 us (3%)
  local copies, waits for them, and re-layouts  2.42 us (2%)
    reduce_scatter x1, waiting for transfers between devices, local(): lax.psum_scatter(forward, 'emit', scatter_dimension=1, tiled=True)  21.6 us
    reduce_scatter x1, waiting for transfers between devices, local(): lax.psum_scatter(adjoint, 'recv', scatter_dimension=1, tiled=True)  20 us
    all_gather x1, blocking collectives, local(): col_geom = lax.all_gather(geometry, 'emit', axis=1, tiled=True)  14.8 us
    all_gather x1, blocking collectives, local(): col_weight = lax.all_gather(own_weights, 'emit', axis=1, tiled=True)  13.1 us
    dot_general x8, matrix products, inner(): jnp.dot(value_part, tile, preferred_element_type=jnp.float32)  6.43 us
    dot_general x8, matrix products, inner(): lax.dot_general(col_weight, tile, (((1,), (1,)), ((), ())), preferred_ele...  6.15 us
    all_gather x1, blocking collectives, local(): row_values = lax.all_gather(own_values, 'recv', axis=1, tiled=True)  5.23 us
    all_gather x1, blocking collectives, local(): geom_piece = lax.all_gather(geometry, 'recv', axis=1, tiled=True)  5.18 us
  transfers between devices with their start and end apart: 2, of which 2 were waited for; matrix products, arithmetic and copies ran while one was open for 0% of the time, Pallas kernels for 0%

commit v1 on v0

v1 whole, which is shorter than its diff:
```python
import functools
import math

import jax
import jax.numpy as jnp
from jax import lax
from jax.experimental import pallas as pl
from jax.experimental.pallas import tpu as pltpu
from jax.sharding import PartitionSpec as P

BLK = 128
MESH = pl.DeviceIdType.MESH
F32 = jnp.float32
BF16 = jnp.bfloat16


def flip(index, number):
    bit = 1
    while bit <= number:
        if number & bit:
            index = index + bit * (1 - 2 * ((index // bit) % 2))
        bit *= 2
    return index


def partner(index, number, count):
    if count & (count - 1) == 0:
        return flip(index, number)
    return lax.rem(index + number, count)


def split3(x):
    one = x.astype(BF16).astype(F32)
    rest = x - one
    two = rest.astype(BF16).astype(F32)
    return one, two, rest - two


def row_stack(x):
    one, two, three = split3(x)
    return jnp.concatenate([one, one, two, two, one, three], axis=0)


def col_stack(x):
    one, two, three = split3(x)
    return jnp.concatenate([one, two, one, two, three, one], axis=0)


def dot(a, b, ca, cb):
    return lax.dot_general(a, b, (((ca,), (cb,)), ((), ())), preferred_element_type=F32)


def emitter_forms(geom):
    q, normal, area = geom[0:3], geom[3:6], geom[6:7]
    zero = jnp.zeros_like(area)
    one = jnp.ones_like(area)
    scale = area * (1.0 / math.pi)
    scaled = normal * scale
    offset = -jnp.sum(scaled * q, axis=0, keepdims=True)
    square = jnp.sum(q * q, axis=0, keepdims=True) + area
    cos_emit = jnp.concatenate([scaled, offset, zero, zero, zero, zero], axis=0)
    cos_recv = jnp.concatenate([q, one, zero, zero, zero, zero], axis=0)
    spread = jnp.concatenate([-2.0 * q, square, one, zero, zero, zero], axis=0)
    return cos_emit, cos_recv, spread


def receiver_forms(geom):
    q, normal, area = geom[0:3], geom[3:6], geom[6:7]
    zero = jnp.zeros_like(area)
    one = jnp.ones_like(area)
    offset = -jnp.sum(normal * q, axis=0, keepdims=True)
    square = jnp.sum(q * q, axis=0, keepdims=True)
    cos_emit = jnp.concatenate([q, one, zero, zero, zero, zero], axis=0)
    cos_recv = jnp.concatenate([normal, offset, zero, zero, zero, zero], axis=0)
    spread = jnp.concatenate([q, one, square, zero, zero, zero], axis=0)
    return cos_emit, cos_recv, spread


def sweep(
    emit_count,
    recv_count,
    pos_ref,
    ang_ref,
    area_ref,
    emis_ref,
    emission_ref,
    rad_ref,
    adj_ref,
    vis_ref,
    inlet_ref,
    weight_ref,
    out_rad,
    out_adj,
    out_grad,
    row_geom,
    col_geom,
    row_val,
    col_wt,
    mask,
    form_a,
    form_b,
    form_s,
    fwd_part,
    fwd_got,
    adj_part,
    adj_got,
    geom_row_send,
    geom_row_recv,
    geom_col_send,
    geom_col_recv,
    val_send,
    val_recv,
    wt_send,
    wt_recv,
    fwd_send,
    fwd_recv,
    ret_send,
    ret_recv,
):
    e = lax.axis_index("emit")
    r = lax.axis_index("recv")
    own = pos_ref.shape[1]
    blocks = own // BLK
    row_total = own * recv_count

    barrier = pltpu.get_barrier_semaphore()
    for k in range(1, recv_count):
        pl.semaphore_signal(
            barrier, inc=1, device_id={"recv": partner(r, k, recv_count)}, device_id_type=MESH
        )
    for k in range(1, emit_count):
        pl.semaphore_signal(
            barrier, inc=1, device_id={"emit": partner(e, k, emit_count)}, device_id_type=MESH
        )

    q = pos_ref[...] - 0.5
    angles = ang_ref[...]
    sines = jnp.sin(angles)
    cosines = jnp.cos(angles)
    geometry = jnp.concatenate(
        [
            q,
            sines[0:1] * cosines[1:2],
            sines[0:1] * sines[1:2],
            cosines[0:1],
            area_ref[...],
            jnp.zeros((1, own), F32),
        ],
        axis=0,
    )
    row_geom[r] = geometry
    col_geom[e] = geometry
    reflect = 1.0 - emis_ref[...]
    row_val[r] = rad_ref[...].astype(BF16)
    col_wt[e] = (reflect * adj_ref[...]).astype(BF16)

    pl.semaphore_wait(barrier, recv_count + emit_count - 2)

    def copies(buf, dst, send, recv, axis, me, count, gather):
        out = []
        for k in range(1, count):
            peer = partner(me, k, count)
            out.append(
                pltpu.make_async_remote_copy(
                    src_ref=buf.at[me if gather else peer],
                    dst_ref=dst.at[me],
                    send_sem=send.at[peer],
                    recv_sem=recv.at[me],
                    device_id={axis: peer},
                    device_id_type=MESH,
                )
            )
        return out

    def arrival(dst, send, recv, axis, peer):
        return pltpu.make_async_remote_copy(
            src_ref=dst.at[peer],
            dst_ref=dst.at[peer],
            send_sem=send.at[peer],
            recv_sem=recv.at[peer],
            device_id={axis: peer},
            device_id_type=MESH,
        )

    row_geom_out = copies(row_geom, row_geom, geom_row_send, geom_row_recv, "recv", r, recv_count, True)
    col_geom_out = copies(col_geom, col_geom, geom_col_send, geom_col_recv, "emit", e, emit_count, True)
    val_out = copies(row_val, row_val, val_send, val_recv, "recv", r, recv_count, True)
    wt_out = copies(col_wt, col_wt, wt_send, wt_recv, "emit", e, emit_count, True)
    for copy in col_geom_out + row_geom_out + wt_out + val_out:
        copy.start()

    patch = (e * recv_count + r) * own + lax.broadcasted_iota(jnp.int32, (own, 1), 0)
    selector = jnp.where(inlet_ref[...] == patch, 1.0, 0.0).astype(BF16)
    weights = weight_ref[...]
    high = weights.astype(BF16)
    low = (weights - high.astype(F32)).astype(BF16)
    out_adj[...] = dot(high, selector, 1, 1) + dot(low, selector, 1, 1)

    all_blocks = vis_ref.shape[1]
    col_blocks = emit_count * blocks
    number = lax.broadcasted_iota(jnp.int32, (col_blocks, all_blocks), 0)
    wanted = (lax.div(number, blocks) * recv_count + r) * blocks + lax.rem(number, blocks)
    chosen = (lax.broadcasted_iota(jnp.int32, (col_blocks, all_blocks), 1) == wanted).astype(F32)
    tile_mask = dot(chosen.astype(BF16), vis_ref[...].astype(F32).astype(BF16), 1, 1)
    row_blocks = recv_count * blocks
    spot = lax.broadcasted_iota(jnp.int32, (row_blocks, row_total), 1) // BLK
    expand = (lax.broadcasted_iota(jnp.int32, (row_blocks, row_total), 0) == spot).astype(F32)
    mask[...] = dot(tile_mask.astype(BF16), expand.astype(BF16), 1, 0)

    for k in range(recv_count):
        peer = partner(r, k, recv_count)
        if k:
            arrival(row_geom, geom_row_send, geom_row_recv, "recv", peer).wait_recv()
        for form, buf in zip(emitter_forms(row_geom[peer]), (form_a, form_b, form_s)):
            buf[peer] = row_stack(form).astype(BF16)

    for k in range(recv_count):
        adj_part[k] = jnp.zeros(adj_part.shape[1:], F32)

    lane = lax.broadcasted_iota(jnp.int32, (1, own), 1) // BLK

    def columns(peer):
        forms = [col_stack(form) for form in receiver_forms(col_geom[peer])]
        spaced = jnp.concatenate([jnp.where(lane == b, forms[0], 0.0) for b in range(blocks)], axis=0)
        side_a = spaced.T.astype(BF16)
        side_b = forms[1].T.astype(BF16)
        side_s = forms[2].T.astype(BF16)
        weight = col_wt[peer]

        def rows(number, total):
            start = pl.multiple_of(number * own, own)
            base = form_a[number]
            masked = jnp.concatenate(
                [
                    base * mask[pl.ds(peer * blocks + b, 1), pl.ds(start, own)].astype(BF16)
                    for b in range(blocks)
                ],
                axis=0,
            )
            cos_emit = jnp.maximum(dot(side_a, masked, 1, 0), 0.0)
            cos_recv = jnp.maximum(dot(side_b, form_b[number], 1, 0), 0.0)
            spread = dot(side_s, form_s[number], 1, 0)
            tile = (cos_emit * cos_recv * pl.reciprocal(spread * spread, approx=True)).astype(BF16)
            adj_part[number] += dot(weight, tile, 1, 0)
            return total + dot(row_val[number], tile, 1, 1)

        zero = jnp.zeros(fwd_part.shape[1:], F32)
        fwd_part[peer] = lax.fori_loop(0, recv_count, rows, zero, unroll=recv_count <= 4)

    for k in range(1, recv_count):
        arrival(row_val, val_send, val_recv, "recv", partner(r, k, recv_count)).wait_recv()

    fwd_out = copies(fwd_part, fwd_got, fwd_send, fwd_recv, "emit", e, emit_count, False)
    columns(e)
    for k in reversed(range(1, emit_count)):
        peer = partner(e, k, emit_count)
        arrival(col_geom, geom_col_send, geom_col_recv, "emit", peer).wait_recv()
        arrival(col_wt, wt_send, wt_recv, "emit", peer).wait_recv()
        columns(peer)
        fwd_out[k - 1].start()

    ret_out = copies(adj_part, adj_got, ret_send, ret_recv, "recv", r, recv_count, False)
    for copy in ret_out:
        copy.start()

    incoming = fwd_part[e]
    for k in range(1, emit_count):
        peer = partner(e, k, emit_count)
        arrival(fwd_got, fwd_send, fwd_recv, "emit", peer).wait_recv()
        incoming = incoming + fwd_got[peer]
    emission = emission_ref[...]
    out_rad[...] = emis_ref[...] * emission + reflect * incoming
    adjoint = out_adj[...] + adj_part[r]
    for k in range(1, recv_count):
        peer = partner(r, k, recv_count)
        arrival(adj_got, ret_send, ret_recv, "recv", peer).wait_recv()
        adjoint = adjoint + adj_got[peer]
    out_adj[...] = adjoint
    out_grad[...] = jnp.sum(adjoint * (emission - incoming), axis=0, keepdims=True)

    for copy in row_geom_out + col_geom_out + val_out + wt_out + fwd_out + ret_out:
        copy.wait_send()


def local(
    positions,
    angles,
    areas,
    emissivity,
    emission,
    radiosity_in,
    adjoint_in,
    visibility,
    inlet_patches,
    inlet_weights,
):
    emit_count = lax.axis_size("emit")
    recv_count = lax.axis_size("recv")
    own = areas.shape[0]
    cases = emission.shape[0]
    blocks = own // BLK
    row_total = own * recv_count
    vmem = pl.BlockSpec(memory_space=pltpu.VMEM)
    emit_sem = pltpu.SemaphoreType.DMA((emit_count,))
    recv_sem = pltpu.SemaphoreType.DMA((recv_count,))
    radiosity_out, adjoint_out, grad = pl.pallas_call(
        functools.partial(sweep, emit_count, recv_count),
        out_shape=(
            jax.ShapeDtypeStruct((cases, own), F32),
            jax.ShapeDtypeStruct((cases, own), F32),
            jax.ShapeDtypeStruct((1, own), F32),
        ),
        in_specs=[vmem] * 10,
        out_specs=(vmem, vmem, vmem),
        scratch_shapes=[
            pltpu.VMEM((recv_count, 8, own), F32),
            pltpu.VMEM((emit_count, 8, own), F32),
            pltpu.VMEM((recv_count, cases, own), BF16),
            pltpu.VMEM((emit_count, cases, own), BF16),
            pltpu.VMEM((emit_count * blocks, row_total), F32),
            pltpu.VMEM((recv_count, 48, own), BF16),
            pltpu.VMEM((recv_count, 48, own), BF16),
            pltpu.VMEM((recv_count, 48, own), BF16),
            pltpu.VMEM((emit_count, cases, own), F32),
            pltpu.VMEM((emit_count, cases, own), F32),
            pltpu.VMEM((recv_count, cases, own), F32),
            pltpu.VMEM((recv_count, cases, own), F32),
            recv_sem,
            recv_sem,
            emit_sem,
            emit_sem,
            recv_sem,
            recv_sem,
            emit_sem,
            emit_sem,
            emit_sem,
            emit_sem,
            recv_sem,
            recv_sem,
        ],
        compiler_params=pltpu.CompilerParams(
            collective_id=0, has_side_effects=True, vmem_limit_bytes=40 * 1024 * 1024
        ),
        name="sweep",
    )(
        positions,
        angles,
        areas[None, :],
        emissivity[None, :],
        emission,
        radiosity_in,
        adjoint_in,
        visibility,
        inlet_patches[None, :],
        inlet_weights,
    )
    return (radiosity_out, adjoint_out, grad[0])


def solution(mesh):
    placed = (
        P(None, ("groups", "emit", "recv")),
        P(None, ("groups", "emit", "recv")),
        P(("groups", "emit", "recv")),
        P(("groups", "emit", "recv")),
        P(None, ("groups", "emit", "recv")),
        P(None, ("groups", "emit", "recv")),
        P(None, ("groups", "emit", "recv")),
        P(("groups", "emit"), None),
        P("groups"),
        P(None, "groups"),
    )
    return jax.shard_map(
        local,
        mesh=mesh,
        in_specs=placed,
        out_specs=(
            P(None, ("groups", "emit", "recv")),
            P(None, ("groups", "emit", "recv")),
            P(("groups", "emit", "recv")),
        ),
        check_vma=False,
    )
```

time: 116 us -> 26.8 us (0.23)
  waiting for transfers between devices: 42.3 us -> 0 us
  blocking collectives: 38.3 us -> 0 us
  Pallas kernels: 0 us -> 17.2 us
  matrix products: 15.3 us -> 0 us
  between operations: 14.1 us -> 0.67 us
  local copies, waits for them, and re-layouts: 2.42 us -> 8.44 us
  other arithmetic: 2.97 us -> 0 us
    reduce_scatter x2 -> x0, waiting for transfers between devices: 41.6 us -> none  [the longest x1 21.6 us: local(): lax.psum_scatter(forward, 'emit', scatter_dimension=1, tiled=True)]
    all_gather x4 -> x0, blocking collectives: 38.3 us -> none  [the longest x1 14.8 us: local(): col_geom = lax.all_gather(geometry, 'emit', axis=1, tiled=True)]
    pallas_call x0 -> x1, Pallas kernels: none -> 17.2 us  [local(): pl.pallas_call(functools.partial(sweep, emit_count, recv_count), out_shap...]
    dot_general x17 -> x0, matrix products: 15.3 us -> none  [the longest x8 6.43 us: inner(): jnp.dot(value_part, tile, preferred_element_type=jnp.float32)]
    unnamed x15 -> x23, local copies, waits for them, and re-layouts: 0.72 us -> 8.44 us
    convert_element_type x3 -> x0, other arithmetic: 1.46 us -> none  [the longest x1 0.76 us: local(): own_values = radiosity_in.astype(jnp.bfloat16)]
  transfers between devices with their start and end apart: 2 -> 0, of which waited for: 2 -> 0; matrix products, arithmetic and copies ran while one was open for 0% -> 0% of each run, Pallas kernels for 0% -> 0%
where the time goes in v1:
time: 26.8 us; the launch traced here: 26.3 us
  Pallas kernels  17.2 us (64%)
  local copies, waits for them, and re-layouts  8.44 us (31%)
  between operations  0.67 us (2%)
    pallas_call x1, Pallas kernels, local(): pl.pallas_call(functools.partial(sweep, emit_count, recv_count), out_shap...  17.2 us
    unnamed x23, local copies, waits for them, and re-layouts  8.44 us

profile of v1, /device:TPU:0, one launch (start us, length us, event | category | flops | bytes accessed | tf_op | source)
XLA Modules:
  0.0 26.3 jit_solution(9801307983225423987)
XLA Ops:
  0.6 0.0 copy-start.5
  0.6 0.0 copy-start.8
  0.7 0.7 %copy-done.5 = f32[3,256]{1,0:T(4,128)S(1)} copy-done((f32[3,256]{1,0:T(4,128)S(1)}, f32[3,256]{1,0:T(4,128)}, u32[]{:S(2)}) %copy-start.5) | copy-done | bytes 3096
  1.3 0.0 copy-done.8
  1.3 0.0 copy-start
  1.3 0.9 %copy-done = f32[32,2048]{1,0:T(8,128)S(1)} copy-done((f32[32,2048]{1,0:T(8,128)S(1)}, f32[32,2048]{1,0:T(8,128)}, u32[]{:S(2)}) %copy-start) | copy-done | bytes 262168
  2.3 0.0 copy-start.1
  2.3 0.8 %copy-done.1 = f32[32,256]{1,0:T(8,128)S(1)} copy-done((f32[32,256]{1,0:T(8,128)S(1)}, f32[32,256]{1,0:T(8,128)}, u32[]{:S(2)}) %copy-start.1) | copy-done | bytes 32792
  3.0 0.0 copy-start.2
  3.0 0.8 %copy-done.2 = f32[32,256]{1,0:T(8,128)S(1)} copy-done((f32[32,256]{1,0:T(8,128)S(1)}, f32[32,256]{1,0:T(8,128)}, u32[]{:S(2)}) %copy-start.2) | copy-done | bytes 32792
  3.8 0.0 copy-start.3
  3.8 0.8 %copy-done.3 = f32[32,256]{1,0:T(8,128)S(1)} copy-done((f32[32,256]{1,0:T(8,128)S(1)}, f32[32,256]{1,0:T(8,128)}, u32[]{:S(2)}) %copy-start.3) | copy-done | bytes 32792
  4.6 0.0 copy-start.4
  4.6 0.7 %copy-done.4 = s32[2048]{0:T(1024)S(1)} copy-done((s32[2048]{0:T(1024)S(1)}, s32[2048]{0:T(1024)}, u32[]{:S(2)}) %copy-start.4) | copy-done | bytes 8216
  5.3 0.0 copy-start.6
  5.3 0.7 %copy-done.6 = s32[8,32]{1,0:T(8,128)S(1)} copy-done((s32[8,32]{1,0:T(8,128)S(1)}, s32[8,32]{1,0:T(8,128)}, u32[]{:S(2)}) %copy-start.6) | copy-done | bytes 1048
  5.9 0.0 copy-start.7
  5.9 0.7 %copy-done.7 = f32[2,256]{1,0:T(2,128)S(1)} copy-done((f32[2,256]{1,0:T(2,128)S(1)}, f32[2,256]{1,0:T(2,128)}, u32[]{:S(2)}) %copy-start.7) | copy-done | bytes 2072
  6.6 0.0 copy-start.9
  6.6 0.7 %copy-done.9 = f32[256]{0:T(256)S(1)} copy-done((f32[256]{0:T(256)S(1)}, f32[256]{0:T(256)}, u32[]{:S(2)}) %copy-start.9) | copy-done | bytes 1048
  7.3 17.2 %sweep.1 = (f32[32,256]{1,0:T(8,128)S(1)}, f32[32,256]{1,0:T(8,128)S(1)}, f32[1,256]{1,0:T(1,128)S(1)}) custom-call(f32[3,256]{1,0:T(4,128)S(1)} %copy-done.5, f32[2,256]{1,0:T(2,128)S(1)} %copy-done.7, f32[1,256]{1,0:T(1,128)S(1)} %bitcast.5, f32[1,256]{1,0:T(1,128)S(1)} %bitcast.6, f32[32,256]{1,0:T(8,128)S(1)} %copy-done.1, f32[32,256]{1,0:T(8,128)S(1)} %copy-done.2, ...), custom_call_target="tpu_custom_call" | custom-call | tf_op jit(solution)/shard_map/sweep/pallas_call | solution.py:306
  24.6 0.6 %copy.16 = f32[32,256]{1,0:T(8,128)} copy(f32[32,256]{1,0:T(8,128)S(1)} %get-tuple-element.12) | data formatting | bytes 65536
  25.2 0.6 %copy.17 = f32[32,256]{1,0:T(8,128)} copy(f32[32,256]{1,0:T(8,128)S(1)} %get-tuple-element.13) | data formatting | bytes 65536
  25.8 0.6 %copy.18 = f32[256]{0:T(256)} copy(f32[256]{0:T(256)S(1)} %bitcast.7) | data formatting | bytes 2048
Async XLA Ops:
  0.6 0.7 %copy-start.5 = (f32[3,256]{1,0:T(4,128)S(1)}, f32[3,256]{1,0:T(4,128)}, u32[]{:S(2)}) copy-start(f32[3,256]{1,0:T(4,128)} %pos_ref.1) | copy-start | bytes 9220
  0.6 0.7 %copy-start.8 = (f32[256]{0:T(256)S(1)}, f32[256]{0:T(256)}, u32[]{:S(2)}) copy-start(f32[256]{0:T(256)} %param.12) | copy-start | bytes 3076
  1.3 0.9 %copy-start = (f32[32,2048]{1,0:T(8,128)S(1)}, f32[32,2048]{1,0:T(8,128)}, u32[]{:S(2)}) copy-start(f32[32,2048]{1,0:T(8,128)} %weight_ref.1) | copy-start | bytes 786436
  2.3 0.8 %copy-start.1 = (f32[32,256]{1,0:T(8,128)S(1)}, f32[32,256]{1,0:T(8,128)}, u32[]{:S(2)}) copy-start(f32[32,256]{1,0:T(8,128)} %emission_ref.1) | copy-start | bytes 98308
  3.0 0.8 %copy-start.2 = (f32[32,256]{1,0:T(8,128)S(1)}, f32[32,256]{1,0:T(8,128)}, u32[]{:S(2)}) copy-start(f32[32,256]{1,0:T(8,128)} %rad_ref.1) | copy-start | bytes 98308
  3.8 0.8 %copy-start.3 = (f32[32,256]{1,0:T(8,128)S(1)}, f32[32,256]{1,0:T(8,128)}, u32[]{:S(2)}) copy-start(f32[32,256]{1,0:T(8,128)} %adj_ref.1) | copy-start | bytes 98308
  4.6 0.7 %copy-start.4 = (s32[2048]{0:T(1024)S(1)}, s32[2048]{0:T(1024)}, u32[]{:S(2)}) copy-start(s32[2048]{0:T(1024)} %param.18) | copy-start | bytes 24580
  5.3 0.7 %copy-start.6 = (s32[8,32]{1,0:T(8,128)S(1)}, s32[8,32]{1,0:T(8,128)}, u32[]{:S(2)}) copy-start(s32[8,32]{1,0:T(8,128)} %vis_ref.1) | copy-start | bytes 3076
  5.9 0.7 %copy-start.7 = (f32[2,256]{1,0:T(2,128)S(1)}, f32[2,256]{1,0:T(2,128)}, u32[]{:S(2)}) copy-start(f32[2,256]{1,0:T(2,128)} %ang_ref.1) | copy-start | bytes 6148
  6.6 0.7 %copy-start.9 = (f32[256]{0:T(256)S(1)}, f32[256]{0:T(256)}, u32[]{:S(2)}) copy-start(f32[256]{0:T(256)} %param.13) | copy-start | bytes 3076

commit v2 on v1

--- a/solution.py
+++ b/solution.py
@@ -79,19 +79,30 @@
 def sweep(
     emit_count,
     recv_count,
+    pos_hbm,
+    ang_hbm,
+    area_hbm,
+    emis_hbm,
+    rad_hbm,
+    adj_hbm,
+    vis_hbm,
+    inlet_hbm,
+    weight_hbm,
+    emission_hbm,
+    out_rad,
+    out_adj,
+    out_grad,
     pos_ref,
     ang_ref,
     area_ref,
     emis_ref,
-    emission_ref,
     rad_ref,
     adj_ref,
     vis_ref,
     inlet_ref,
     weight_ref,
-    out_rad,
-    out_adj,
-    out_grad,
+    emission_ref,
+    load_sem,
     row_geom,
     col_geom,
     row_val,
@@ -133,6 +144,28 @@
             barrier, inc=1, device_id={"emit": partner(e, k, emit_count)}, device_id_type=MESH
         )
 
+    loads = [
+        pltpu.make_async_copy(src, dst, load_sem.at[number])
+        for number, (src, dst) in enumerate(
+            (
+                (pos_hbm, pos_ref),
+                (ang_hbm, ang_ref),
+                (area_hbm, area_ref),
+                (emis_hbm, emis_ref),
+                (rad_hbm, rad_ref),
+                (adj_hbm, adj_ref),
+                (vis_hbm, vis_ref),
+                (inlet_hbm, inlet_ref),
+                (weight_hbm, weight_ref),
+                (emission_hbm, emission_ref),
+            )
+        )
+    ]
+    for load in loads:
+        load.start()
+
+    for load in loads[:3]:
+        load.wait()
     q = pos_ref[...] - 0.5
     angles = ang_ref[...]
     sines = jnp.sin(angles)
@@ -150,10 +183,6 @@
     )
     row_geom[r] = geometry
     col_geom[e] = geometry
-    reflect = 1.0 - emis_ref[...]
-    row_val[r] = rad_ref[...].astype(BF16)
-    col_wt[e] = (reflect * adj_ref[...]).astype(BF16)
-
     pl.semaphore_wait(barrier, recv_count + emit_count - 2)
 
     def copies(buf, dst, send, recv, axis, me, count, gather):
@@ -184,18 +213,18 @@
 
     row_geom_out = copies(row_geom, row_geom, geom_row_send, geom_row_recv, "recv", r, recv_count, True)
     col_geom_out = copies(col_geom, col_geom, geom_col_send, geom_col_recv, "emit", e, emit_count, True)
+    for copy in col_geom_out + row_geom_out:
+        copy.start()
+    for load in loads[3:6]:
+        load.wait()
+    row_val[r] = rad_ref[...].astype(BF16)
+    col_wt[e] = ((1.0 - emis_ref[...]) * adj_ref[...]).astype(BF16)
     val_out = copies(row_val, row_val, val_send, val_recv, "recv", r, recv_count, True)
     wt_out = copies(col_wt, col_wt, wt_send, wt_recv, "emit", e, emit_count, True)
-    for copy in col_geom_out + row_geom_out + wt_out + val_out:
+    for copy in wt_out + val_out:
         copy.start()
 
-    patch = (e * recv_count + r) * own + lax.broadcasted_iota(jnp.int32, (own, 1), 0)
-    selector = jnp.where(inlet_ref[...] == patch, 1.0, 0.0).astype(BF16)
-    weights = weight_ref[...]
-    high = weights.astype(BF16)
-    low = (weights - high.astype(F32)).astype(BF16)
-    out_adj[...] = dot(high, selector, 1, 1) + dot(low, selector, 1, 1)
-
+    loads[6].wait()
     all_blocks = vis_ref.shape[1]
     col_blocks = emit_count * blocks
     number = lax.broadcasted_iota(jnp.int32, (col_blocks, all_blocks), 0)
@@ -263,23 +292,46 @@
     for copy in ret_out:
         copy.start()
 
+    for load in loads[7:]:
+        load.wait()
+    patch = (e * recv_count + r) * own + lax.broadcasted_iota(jnp.int32, (own, 1), 0)
+    selector = jnp.where(inlet_ref[...] == patch, 1.0, 0.0).astype(BF16)
+    weights = weight_ref[...]
+    high = weights.astype(BF16)
+    low = (weights - high.astype(F32)).astype(BF16)
+    source = dot(high, selector, 1, 1) + dot(low, selector, 1, 1)
+
     incoming = fwd_part[e]
     for k in range(1, emit_count):
         peer = partner(e, k, emit_count)
         arrival(fwd_got, fwd_send, fwd_recv, "emit", peer).wait_recv()
         incoming = incoming + fwd_got[peer]
     emission = emission_ref[...]
-    out_rad[...] = emis_ref[...] * emission + reflect * incoming
-    adjoint = out_adj[...] + adj_part[r]
+    share = emis_ref[...]
+    out_rad[...] = share * emission + (1.0 - share) * incoming
+    returned = adj_part[r]
     for k in range(1, recv_count):
         peer = partner(r, k, recv_count)
         arrival(adj_got, ret_send, ret_recv, "recv", peer).wait_recv()
-        adjoint = adjoint + adj_got[peer]
+        returned = returned + adj_got[peer]
+    adjoint = source + returned
     out_adj[...] = adjoint
     out_grad[...] = jnp.sum(adjoint * (emission - incoming), axis=0, keepdims=True)
 
     for copy in row_geom_out + col_geom_out + val_out + wt_out + fwd_out + ret_out:
         copy.wait_send()
+
+
+def finish(rad_ref, adj_ref, grad_ref, rad_hbm, adj_hbm, grad_hbm, sem):
+    stores = [
+        pltpu.make_async_copy(rad_ref, rad_hbm, sem.at[0]),
+        pltpu.make_async_copy(adj_ref, adj_hbm, sem.at[1]),
+        pltpu.make_async_copy(grad_ref, grad_hbm, sem.at[2]),
+    ]
+    for copy in stores:
+        copy.start()
+    for copy in stores:
+        copy.wait()
 
 
 def local(
@@ -301,18 +353,31 @@
     blocks = own // BLK
     row_total = own * recv_count
     vmem = pl.BlockSpec(memory_space=pltpu.VMEM)
+    hbm = pl.BlockSpec(memory_space=pltpu.HBM)
     emit_sem = pltpu.SemaphoreType.DMA((emit_count,))
     recv_sem = pltpu.SemaphoreType.DMA((recv_count,))
-    radiosity_out, adjoint_out, grad = pl.pallas_call(
+    operands = (
+        positions,
+        angles,
+        areas[None, :],
+        emissivity[None, :],
+        radiosity_in,
+        adjoint_in,
+        visibility,
+        inlet_patches[None, :],
+        inlet_weights,
+        emission,
+    )
+    flat = jax.ShapeDtypeStruct((cases, own), F32)
+    results = (flat, flat, jax.ShapeDtypeStruct((1, own), F32))
+    swept = pl.pallas_call(
         functools.partial(sweep, emit_count, recv_count),
-        out_shape=(
-            jax.ShapeDtypeStruct((cases, own), F32),
-            jax.ShapeDtypeStruct((cases, own), F32),
-            jax.ShapeDtypeStruct((1, own), F32),
-        ),
-        in_specs=[vmem] * 10,
+        out_shape=results,
+        in_specs=[hbm] * len(operands),
         out_specs=(vmem, vmem, vmem),
-        scratch_shapes=[
+        scratch_shapes=[pltpu.VMEM(x.shape, x.dtype) for x in operands]
+        + [
+            pltpu.SemaphoreType.DMA((len(operands),)),
             pltpu.VMEM((recv_count, 8, own), F32),
             pltpu.VMEM((emit_count, 8, own), F32),
             pltpu.VMEM((recv_count, cases, own), BF16),
@@ -342,18 +407,15 @@
             collective_id=0, has_side_effects=True, vmem_limit_bytes=40 * 1024 * 1024
         ),
         name="sweep",
-    )(
-        positions,
-        angles,
-        areas[None, :],
-        emissivity[None, :],
-        emission,
-        radiosity_in,
-        adjoint_in,
-        visibility,
-        inlet_patches[None, :],
-        inlet_weights,
-    )
+    )(*operands)
+    radiosity_out, adjoint_out, grad = pl.pallas_call(
+        finish,
+        out_shape=results,
+        in_specs=[vmem, vmem, vmem],
+        out_specs=(hbm, hbm, hbm),
+        scratch_shapes=[pltpu.SemaphoreType.DMA((3,))],
+        name="finish",
+    )(*swept)
     return (radiosity_out, adjoint_out, grad[0])
 
 

time: 26.8 us -> 28.6 us (1.067)
  Pallas kernels: 17.2 us -> 18.9 us
    pallas_call x0 -> x1, Pallas kernels: none -> 1.43 us  [local(): pl.pallas_call(finish, out_shape=results, in_specs=[vmem, vmem, vmem], ou...]
    unnamed x23 -> x26, local copies, waits for them, and re-layouts: 8.44 us -> 8.44 us
where the time goes in v2:
time: 28.6 us; the launch traced here: 28 us
  Pallas kernels  18.9 us (66%)
  local copies, waits for them, and re-layouts  8.44 us (30%)
  between operations  0.68 us (2%)
    pallas_call x1, Pallas kernels, local(): pl.pallas_call(functools.partial(sweep, emit_count, recv_count), out_shap...  17.5 us
    unnamed x26, local copies, waits for them, and re-layouts  8.44 us
    pallas_call x1, Pallas kernels, local(): pl.pallas_call(finish, out_shape=results, in_specs=[vmem, vmem, vmem], ou...  1.43 us

profile of v2, /device:TPU:0, one launch (start us, length us, event | category | flops | bytes accessed | tf_op | source)
XLA Modules:
  0.0 28.0 jit_solution(8784377683340814327)
XLA Ops:
  0.6 0.0 copy-start.7
  0.6 0.0 copy-start.10
  0.7 0.7 %copy-done.7 = f32[3,256]{1,0:T(4,128)S(1)} copy-done((f32[3,256]{1,0:T(4,128)S(1)}, f32[3,256]{1,0:T(4,128)}, u32[]{:S(2)}) %copy-start.7) | copy-done | bytes 3096
  1.3 0.0 copy-done.10
  1.3 0.0 copy-start
  1.3 0.9 %copy-done = f32[32,2048]{1,0:T(8,128)S(1)} copy-done((f32[32,2048]{1,0:T(8,128)S(1)}, f32[32,2048]{1,0:T(8,128)}, u32[]{:S(2)}) %copy-start) | copy-done | bytes 262168
  2.3 0.0 copy-start.1
  2.3 0.8 %copy-done.1 = f32[32,256]{1,0:T(8,128)S(1)} copy-done((f32[32,256]{1,0:T(8,128)S(1)}, f32[32,256]{1,0:T(8,128)}, u32[]{:S(2)}) %copy-start.1) | copy-done | bytes 32792
  3.0 0.8 %copy-done.2 = f32[32,256]{1,0:T(8,128)S(1)} copy-done((f32[32,256]{1,0:T(8,128)S(1)}, f32[32,256]{1,0:T(8,128)}, u32[]{:S(2)}) %copy-start.2) | copy-done | bytes 32792
  3.8 0.0 copy-start.3
  3.8 0.8 %copy-done.3 = f32[32,256]{1,0:T(8,128)S(1)} copy-done((f32[32,256]{1,0:T(8,128)S(1)}, f32[32,256]{1,0:T(8,128)}, u32[]{:S(2)}) %copy-start.3) | copy-done | bytes 32792
  4.6 0.0 copy-start.6
  4.6 0.7 %copy-done.6 = s32[2048]{0:T(1024)S(1)} copy-done((s32[2048]{0:T(1024)S(1)}, s32[2048]{0:T(1024)}, u32[]{:S(2)}) %copy-start.6) | copy-done | bytes 8216
  5.3 0.0 copy-start.8
  5.3 0.7 %copy-done.8 = s32[8,32]{1,0:T(8,128)S(1)} copy-done((s32[8,32]{1,0:T(8,128)S(1)}, s32[8,32]{1,0:T(8,128)}, u32[]{:S(2)}) %copy-start.8) | copy-done | bytes 1048
  5.9 0.0 copy-start.9
  5.9 0.7 %copy-done.9 = f32[2,256]{1,0:T(2,128)S(1)} copy-done((f32[2,256]{1,0:T(2,128)S(1)}, f32[2,256]{1,0:T(2,128)}, u32[]{:S(2)}) %copy-start.9) | copy-done | bytes 2072
  6.6 0.7 %copy-done.11 = f32[256]{0:T(256)S(1)} copy-done((f32[256]{0:T(256)S(1)}, f32[256]{0:T(256)}, u32[]{:S(2)}) %copy-start.11) | copy-done | bytes 1048
  7.3 17.5 %sweep.1 = (f32[32,256]{1,0:T(8,128)S(1)}, f32[32,256]{1,0:T(8,128)S(1)}, f32[1,256]{1,0:T(1,128)S(1)}) custom-call(f32[3,256]{1,0:T(4,128)S(1)} %copy-done.7, f32[2,256]{1,0:T(2,128)S(1)} %copy-done.9, f32[1,256]{1,0:T(1,128)S(1)} %bitcast.5, f32[1,256]{1,0:T(1,128)S(1)} %bitcast.6, f32[32,256]{1,0:T(8,128)S(1)} %copy-done.1, f32[32,256]{1,0:T(8,128)S(1)} %copy-done.2, ...), custom_call_target="tpu_custom_call" | custom-call | tf_op jit(solution)/shard_map/sweep/pallas_call | solution.py:373
  24.8 0.0 copy-start.4
  24.8 0.6 %copy-done.4 = f32[32,256]{1,0:T(8,128)} copy-done((f32[32,256]{1,0:T(8,128)}, f32[32,256]{1,0:T(8,128)S(1)}, u32[]{:S(2)}) %copy-start.4) | copy-done | bytes 32792
  25.4 0.6 %copy-done.5 = f32[32,256]{1,0:T(8,128)} copy-done((f32[32,256]{1,0:T(8,128)}, f32[32,256]{1,0:T(8,128)S(1)}, u32[]{:S(2)}) %copy-start.5) | copy-done | bytes 32792
  26.0 0.6 %copy-done.12 = f32[1,256]{1,0:T(1,128)} copy-done((f32[1,256]{1,0:T(1,128)}, f32[1,256]{1,0:T(1,128)S(1)}, u32[]{:S(2)}) %copy-start.12) | copy-done | bytes 1048
  26.6 1.4 %finish.1 = (f32[32,256]{1,0:T(8,128)}, f32[32,256]{1,0:T(8,128)}, f32[1,256]{1,0:T(1,128)}) custom-call(f32[32,256]{1,0:T(8,128)} %copy-done.4, f32[32,256]{1,0:T(8,128)} %copy-done.5, f32[1,256]{1,0:T(1,128)} %copy-done.12), custom_call_target="tpu_custom_call" | custom-call | tf_op jit(solution)/shard_map/finish/pallas_call | solution.py:411
  (4 shorter events, 0.0 us)
Async XLA Ops:
  0.6 0.7 %copy-start.7 = (f32[3,256]{1,0:T(4,128)S(1)}, f32[3,256]{1,0:T(4,128)}, u32[]{:S(2)}) copy-start(f32[3,256]{1,0:T(4,128)} %pos_hbm.1) | copy-start | bytes 9220
  0.6 0.7 %copy-start.10 = (f32[256]{0:T(256)S(1)}, f32[256]{0:T(256)}, u32[]{:S(2)}) copy-start(f32[256]{0:T(256)} %param.12) | copy-start | bytes 3076
  1.3 0.9 %copy-start = (f32[32,2048]{1,0:T(8,128)S(1)}, f32[32,2048]{1,0:T(8,128)}, u32[]{:S(2)}) copy-start(f32[32,2048]{1,0:T(8,128)} %weight_hbm.1) | copy-start | bytes 786436
  2.3 0.8 %copy-start.1 = (f32[32,256]{1,0:T(8,128)S(1)}, f32[32,256]{1,0:T(8,128)}, u32[]{:S(2)}) copy-start(f32[32,256]{1,0:T(8,128)} %rad_hbm.1) | copy-start | bytes 98308
  3.0 0.8 %copy-start.2 = (f32[32,256]{1,0:T(8,128)S(1)}, f32[32,256]{1,0:T(8,128)}, u32[]{:S(2)}) copy-start(f32[32,256]{1,0:T(8,128)} %adj_hbm.1) | copy-start | bytes 98308
  3.8 0.8 %copy-start.3 = (f32[32,256]{1,0:T(8,128)S(1)}, f32[32,256]{1,0:T(8,128)}, u32[]{:S(2)}) copy-start(f32[32,256]{1,0:T(8,128)} %emission_hbm.1) | copy-start | bytes 98308
  4.6 0.7 %copy-start.6 = (s32[2048]{0:T(1024)S(1)}, s32[2048]{0:T(1024)}, u32[]{:S(2)}) copy-start(s32[2048]{0:T(1024)} %param.18) | copy-start | bytes 24580
  5.3 0.7 %copy-start.8 = (s32[8,32]{1,0:T(8,128)S(1)}, s32[8,32]{1,0:T(8,128)}, u32[]{:S(2)}) copy-start(s32[8,32]{1,0:T(8,128)} %vis_hbm.1) | copy-start | bytes 3076
  5.9 0.7 %copy-start.9 = (f32[2,256]{1,0:T(2,128)S(1)}, f32[2,256]{1,0:T(2,128)}, u32[]{:S(2)}) copy-start(f32[2,256]{1,0:T(2,128)} %ang_hbm.1) | copy-start | bytes 6148
  6.6 0.7 %copy-start.11 = (f32[256]{0:T(256)S(1)}, f32[256]{0:T(256)}, u32[]{:S(2)}) copy-start(f32[256]{0:T(256)} %param.13) | copy-start | bytes 3076
  24.8 0.6 %copy-start.4 = (f32[32,256]{1,0:T(8,128)}, f32[32,256]{1,0:T(8,128)S(1)}, u32[]{:S(2)}) copy-start(f32[32,256]{1,0:T(8,128)S(1)} %get-tuple-element.9.rad_ref) | copy-start | bytes 98308
  25.4 0.6 %copy-start.5 = (f32[32,256]{1,0:T(8,128)}, f32[32,256]{1,0:T(8,128)S(1)}, u32[]{:S(2)}) copy-start(f32[32,256]{1,0:T(8,128)S(1)} %get-tuple-element.10.adj_ref) | copy-start | bytes 98308
  26.0 0.6 %copy-start.12 = (f32[1,256]{1,0:T(1,128)}, f32[1,256]{1,0:T(1,128)S(1)}, u32[]{:S(2)}) copy-start(f32[1,256]{1,0:T(1,128)S(1)} %get-tuple-element.11.grad_ref) | copy-start | bytes 3076

commit v3 on v2

--- a/solution.py
+++ b/solution.py
@@ -89,9 +89,11 @@
     inlet_hbm,
     weight_hbm,
     emission_hbm,
-    out_rad,
-    out_adj,
-    out_grad,
+    own_hbm,
+    lit_hbm,
+    diff_hbm,
+    src_hbm,
+    ret_hbm,
     pos_ref,
     ang_ref,
     area_ref,
@@ -102,7 +104,13 @@
     inlet_ref,
     weight_ref,
     emission_ref,
+    out_own,
+    out_lit,
+    out_diff,
+    out_src,
+    out_ret,
     load_sem,
+    store_sem,
     row_geom,
     col_geom,
     row_val,
@@ -161,6 +169,18 @@
             )
         )
     ]
+    stores = [
+        pltpu.make_async_copy(src, dst, store_sem.at[number])
+        for number, (src, dst) in enumerate(
+            (
+                (out_own, own_hbm),
+                (out_src, src_hbm),
+                (out_lit, lit_hbm),
+                (out_diff, diff_hbm),
+                (out_ret, ret_hbm),
+            )
+        )
+    ]
     for load in loads:
         load.start()
 
@@ -299,37 +319,33 @@
     weights = weight_ref[...]
     high = weights.astype(BF16)
     low = (weights - high.astype(F32)).astype(BF16)
-    source = dot(high, selector, 1, 1) + dot(low, selector, 1, 1)
+    out_src[...] = dot(high, selector, 1, 1) + dot(low, selector, 1, 1)
+
+    stores[1].start()
+    share = emis_ref[...]
+    emission = emission_ref[...]
+    out_own[...] = share * emission
+    stores[0].start()
 
     incoming = fwd_part[e]
     for k in range(1, emit_count):
         peer = partner(e, k, emit_count)
         arrival(fwd_got, fwd_send, fwd_recv, "emit", peer).wait_recv()
         incoming = incoming + fwd_got[peer]
-    emission = emission_ref[...]
-    share = emis_ref[...]
-    out_rad[...] = share * emission + (1.0 - share) * incoming
+    out_lit[...] = (1.0 - share) * incoming
+    stores[2].start()
+    out_diff[...] = emission - incoming
+    stores[3].start()
     returned = adj_part[r]
     for k in range(1, recv_count):
         peer = partner(r, k, recv_count)
         arrival(adj_got, ret_send, ret_recv, "recv", peer).wait_recv()
         returned = returned + adj_got[peer]
-    adjoint = source + returned
-    out_adj[...] = adjoint
-    out_grad[...] = jnp.sum(adjoint * (emission - incoming), axis=0, keepdims=True)
+    out_ret[...] = returned
+    stores[4].start()
 
     for copy in row_geom_out + col_geom_out + val_out + wt_out + fwd_out + ret_out:
         copy.wait_send()
-
-
-def finish(rad_ref, adj_ref, grad_ref, rad_hbm, adj_hbm, grad_hbm, sem):
-    stores = [
-        pltpu.make_async_copy(rad_ref, rad_hbm, sem.at[0]),
-        pltpu.make_async_copy(adj_ref, adj_hbm, sem.at[1]),
-        pltpu.make_async_copy(grad_ref, grad_hbm, sem.at[2]),
-    ]
-    for copy in stores:
-        copy.start()
     for copy in stores:
         copy.wait()
 
@@ -352,7 +368,6 @@
     cases = emission.shape[0]
     blocks = own // BLK
     row_total = own * recv_count
-    vmem = pl.BlockSpec(memory_space=pltpu.VMEM)
     hbm = pl.BlockSpec(memory_space=pltpu.HBM)
     emit_sem = pltpu.SemaphoreType.DMA((emit_count,))
     recv_sem = pltpu.SemaphoreType.DMA((recv_count,))
@@ -369,15 +384,16 @@
         emission,
     )
     flat = jax.ShapeDtypeStruct((cases, own), F32)
-    results = (flat, flat, jax.ShapeDtypeStruct((1, own), F32))
-    swept = pl.pallas_call(
+    emitted, lit, difference, source, returned = pl.pallas_call(
         functools.partial(sweep, emit_count, recv_count),
-        out_shape=results,
+        out_shape=(flat,) * 5,
         in_specs=[hbm] * len(operands),
-        out_specs=(vmem, vmem, vmem),
+        out_specs=(hbm,) * 5,
         scratch_shapes=[pltpu.VMEM(x.shape, x.dtype) for x in operands]
+        + [pltpu.VMEM((cases, own), F32)] * 5
         + [
             pltpu.SemaphoreType.DMA((len(operands),)),
+            pltpu.SemaphoreType.DMA((5,)),
             pltpu.VMEM((recv_count, 8, own), F32),
             pltpu.VMEM((emit_count, 8, own), F32),
             pltpu.VMEM((recv_count, cases, own), BF16),
@@ -404,19 +420,14 @@
             recv_sem,
         ],
         compiler_params=pltpu.CompilerParams(
-            collective_id=0, has_side_effects=True, vmem_limit_bytes=40 * 1024 * 1024
+            collective_id=0, has_side_effects=True, vmem_limit_bytes=64 * 1024 * 1024
         ),
         name="sweep",
     )(*operands)
-    radiosity_out, adjoint_out, grad = pl.pallas_call(
-        finish,
-        out_shape=results,
-        in_specs=[vmem, vmem, vmem],
-        out_specs=(hbm, hbm, hbm),
-        scratch_shapes=[pltpu.SemaphoreType.DMA((3,))],
-        name="finish",
-    )(*swept)
-    return (radiosity_out, adjoint_out, grad[0])
+    radiosity_out = emitted + lit
+    adjoint_out = source + returned
+    grad = jnp.sum(adjoint_out * difference, axis=0)
+    return (radiosity_out, adjoint_out, grad)
 
 
 def solution(mesh):

time: 28.6 us -> 21.7 us (0.76); the launches traced: 28 us -> 21.5 us
  local copies, waits for them, and re-layouts: 8.44 us -> 0.01 us
  other arithmetic: 0 us -> 2.6 us
  Pallas kernels: 18.9 us -> 18.2 us
    unnamed x26 -> x6, local copies, waits for them, and re-layouts: 8.44 us -> 0.01 us
    pallas_call x1 -> x0, Pallas kernels: 1.43 us -> none  [local(): pl.pallas_call(finish, out_shape=results, in_specs=[vmem, vmem, vmem], ou...]
    add x0 -> x1, other arithmetic: none -> 1.41 us  [local(): radiosity_out = emitted + lit]
    reduce_sum x0 -> x1, other arithmetic: none -> 1.19 us  [local(): grad = jnp.sum(adjoint_out * difference, axis=0)]
    pallas_call x1, Pallas kernels: 17.5 us -> 18.2 us  [local(): pl.pallas_call(functools.partial(sweep, emit_count, recv_count), out_shap...]
where the time goes in v3:
time: 21.7 us; the launch traced here: 21.5 us
  Pallas kernels  18.2 us (84%)
  other arithmetic  2.6 us (12%)
  between operations  0.67 us (3%)
    pallas_call x1, Pallas kernels, local(): pl.pallas_call(functools.partial(sweep, emit_count, recv_count), out_shap...  18.2 us
    add x1, other arithmetic, local(): radiosity_out = emitted + lit  1.41 us
    reduce_sum x1, other arithmetic, local(): grad = jnp.sum(adjoint_out * difference, axis=0)  1.19 us

profile of v3, /device:TPU:0, one launch (start us, length us, event | category | flops | bytes accessed | tf_op | source)
XLA Modules:
  0.0 21.5 jit_solution(15372800910256152695)
XLA Ops:
  0.6 18.2 %sweep.1 = (f32[32,256]{1,0:T(8,128)}, f32[32,256]{1,0:T(8,128)}, f32[32,256]{1,0:T(8,128)}, f32[32,256]{1,0:T(8,128)}, f32[32,256]{1,0:T(8,128)}) custom-call(f32[3,256]{1,0:T(4,128)} %pos_hbm.1, f32[2,256]{1,0:T(2,128)} %ang_hbm.1, f32[1,256]{1,0:T(1,128)} %bitcast.4, f32[1,256]{1,0:T(1,128)} %bitcast.5, f32[32,256]{1,0:T(8,128)} %rad_hbm.1, ...), custom_call_target="tpu_custom_call" | custom-call | tf_op jit(solution)/shard_map/sweep/pallas_call | solution.py:387
  18.8 0.0 copy-start
  18.8 0.0 copy-start.1
  18.9 0.0 copy-start.2
  18.9 1.4 %add.6 = f32[32,256]{1,0:T(8,128)} add(f32[32,256]{1,0:T(8,128)} %get-tuple-element.8, f32[32,256]{1,0:T(8,128)} %get-tuple-element.9) | non-fusion elementwise | flops 8192 | bytes 98304 | tf_op jit(solution)/shard_map/add | solution.py:427
  20.3 0.0 copy-done
  20.3 0.0 copy-done.1
  20.3 0.0 copy-done.2
  20.3 1.2 %multiply_reduce_fusion = (f32[256]{0:T(256)}, f32[32,256]{1,0:T(8,128)}) fusion(f32[32,256]{1,0:T(8,128)S(1)} %copy-done, f32[32,256]{1,0:T(8,128)S(1)} %copy-done.1, f32[32,256]{1,0:T(8,128)S(1)} %copy-done.2), kind=kLoop, calls=%fused_computation | loop fusion | flops 24320 | bytes 132096 | tf_op jit(solution)/shard_map/reduce_sum | solution.py:429
Async XLA Ops:
  18.8 1.4 %copy-start = (f32[32,256]{1,0:T(8,128)S(1)}, f32[32,256]{1,0:T(8,128)}, u32[]{:S(2)}) copy-start(f32[32,256]{1,0:T(8,128)} %get-tuple-element.12) | copy-start | bytes 98308
  18.8 1.4 %copy-start.1 = (f32[32,256]{1,0:T(8,128)S(1)}, f32[32,256]{1,0:T(8,128)}, u32[]{:S(2)}) copy-start(f32[32,256]{1,0:T(8,128)} %get-tuple-element.10) | copy-start | bytes 98308
  18.9 1.4 %copy-start.2 = (f32[32,256]{1,0:T(8,128)S(1)}, f32[32,256]{1,0:T(8,128)}, u32[]{:S(2)}) copy-start(f32[32,256]{1,0:T(8,128)} %get-tuple-element.11) | copy-start | bytes 98308

commit v4 on v2

--- a/solution.py
+++ b/solution.py
@@ -36,44 +36,65 @@
     return one, two, rest - two
 
 
-def row_stack(x):
-    one, two, three = split3(x)
-    return jnp.concatenate([one, one, two, two, one, three], axis=0)
-
-
-def col_stack(x):
-    one, two, three = split3(x)
-    return jnp.concatenate([one, two, one, two, three, one], axis=0)
-
-
 def dot(a, b, ca, cb):
     return lax.dot_general(a, b, (((ca,), (cb,)), ((), ())), preferred_element_type=F32)
 
 
-def emitter_forms(geom):
-    q, normal, area = geom[0:3], geom[3:6], geom[6:7]
-    zero = jnp.zeros_like(area)
-    one = jnp.ones_like(area)
-    scale = area * (1.0 / math.pi)
-    scaled = normal * scale
-    offset = -jnp.sum(scaled * q, axis=0, keepdims=True)
-    square = jnp.sum(q * q, axis=0, keepdims=True) + area
-    cos_emit = jnp.concatenate([scaled, offset, zero, zero, zero, zero], axis=0)
-    cos_recv = jnp.concatenate([q, one, zero, zero, zero, zero], axis=0)
-    spread = jnp.concatenate([-2.0 * q, square, one, zero, zero, zero], axis=0)
-    return cos_emit, cos_recv, spread
-
-
-def receiver_forms(geom):
-    q, normal, area = geom[0:3], geom[3:6], geom[6:7]
-    zero = jnp.zeros_like(area)
-    one = jnp.ones_like(area)
+def sine_cosine(angles):
+    half = 0.5 * angles
+    square = half * half
+    sine = jnp.full_like(half, 1.0 / math.factorial(13))
+    cosine = jnp.full_like(half, 1.0 / math.factorial(14))
+    cosine = cosine * square - 1.0 / math.factorial(12)
+    for order in (11, 9, 7, 5, 3, 1):
+        sign = -1.0 if order % 4 == 3 else 1.0
+        sine = sine * square + sign / math.factorial(order)
+        cosine = cosine * square - sign / math.factorial(order - 1)
+    sine = sine * half
+    cosine = -cosine
+    return 2.0 * sine * cosine, 1.0 - 2.0 * sine * sine
+
+
+def own_blocks_of(q, angles, area):
+    sines, cosines = sine_cosine(angles)
+    normal = jnp.concatenate(
+        [sines[0:1] * cosines[1:2], sines[0:1] * sines[1:2], cosines[0:1]], axis=0
+    )
     offset = -jnp.sum(normal * q, axis=0, keepdims=True)
     square = jnp.sum(q * q, axis=0, keepdims=True)
-    cos_emit = jnp.concatenate([q, one, zero, zero, zero, zero], axis=0)
-    cos_recv = jnp.concatenate([normal, offset, zero, zero, zero, zero], axis=0)
-    spread = jnp.concatenate([q, one, square, zero, zero, zero], axis=0)
-    return cos_emit, cos_recv, spread
+    scale = area * (1.0 / math.pi)
+    emitter = jnp.concatenate([normal * scale, offset * scale, q, square + area], axis=0)
+    receiver = jnp.concatenate([normal, offset, q, square], axis=0)
+    return emitter, receiver
+
+
+def emitter_forms(block):
+    parts = split3(block)
+    row = lax.broadcasted_iota(jnp.int32, block.shape, 0)
+    order = (0, 0, 1, 1, 0, 2)
+    stacks = []
+    for place in (None, 7, 3):
+        form = parts
+        if place is not None:
+            form = [jnp.where(row == place, float(n == 0), part) for n, part in enumerate(parts)]
+        stacks.append(jnp.concatenate([form[n] for n in order], axis=0))
+    return stacks
+
+
+def receiver_forms(block):
+    row = lax.broadcasted_iota(jnp.int32, block.shape, 0)
+    turned = jnp.concatenate([block[4:8], block[0:4]], axis=0)
+    cos_emit, cos_recv, spread = [], [], []
+    for n, (part, swapped) in enumerate(zip(split3(block), split3(turned))):
+        one = float(n == 0)
+        cos_emit.append(jnp.where(row < 3, swapped, jnp.where(row == 3, one, 0.0)))
+        cos_recv.append(jnp.where(row >= 4, swapped, 0.0))
+        inner = jnp.where(row == 7, one, -2.0 * part)
+        spread.append(jnp.where(row == 3, swapped, jnp.where(row >= 4, inner, 0.0)))
+    order = (0, 1, 0, 1, 2, 0)
+    return [
+        jnp.concatenate([form[n] for n in order], axis=0) for form in (cos_emit, cos_recv, spread)
+    ]
 
 
 def sweep(
@@ -89,9 +110,9 @@
     inlet_hbm,
     weight_hbm,
     emission_hbm,
-    out_rad,
-    out_adj,
-    out_grad,
+    rad_out_hbm,
+    adj_out_hbm,
+    grad_out_hbm,
     pos_ref,
     ang_ref,
     area_ref,
@@ -102,7 +123,11 @@
     inlet_ref,
     weight_ref,
     emission_ref,
+    out_rad,
+    out_adj,
+    out_grad,
     load_sem,
+    store_sem,
     row_geom,
     col_geom,
     row_val,
@@ -111,6 +136,8 @@
     form_a,
     form_b,
     form_s,
+    tile,
+    value_t,
     fwd_part,
     fwd_got,
     adj_part,
@@ -161,28 +188,25 @@
             )
         )
     ]
+    stores = [
+        pltpu.make_async_copy(src, dst, store_sem.at[number])
+        for number, (src, dst) in enumerate(
+            (
+                (out_rad, rad_out_hbm),
+                (out_adj, adj_out_hbm),
+                (out_grad, grad_out_hbm),
+            )
+        )
+    ]
     for load in loads:
         load.start()
 
     for load in loads[:3]:
         load.wait()
-    q = pos_ref[...] - 0.5
-    angles = ang_ref[...]
-    sines = jnp.sin(angles)
-    cosines = jnp.cos(angles)
-    geometry = jnp.concatenate(
-        [
-            q,
-            sines[0:1] * cosines[1:2],
-            sines[0:1] * sines[1:2],
-            cosines[0:1],
-            area_ref[...],
-            jnp.zeros((1, own), F32),
-        ],
-        axis=0,
-    )
-    row_geom[r] = geometry
-    col_geom[e] = geometry
+    emitter, receiver = own_blocks_of(pos_ref[...] - 0.5, ang_ref[...], area_ref[...])
+    row_geom[r] = emitter
+    col_geom[e] = receiver
+
     pl.semaphore_wait(barrier, recv_count + emit_count - 2)
 
     def copies(buf, dst, send, recv, axis, me, count, gather):
@@ -241,51 +265,66 @@
         if k:
             arrival(row_geom, geom_row_send, geom_row_recv, "recv", peer).wait_recv()
         for form, buf in zip(emitter_forms(row_geom[peer]), (form_a, form_b, form_s)):
-            buf[peer] = row_stack(form).astype(BF16)
-
-    for k in range(recv_count):
-        adj_part[k] = jnp.zeros(adj_part.shape[1:], F32)
+            buf[peer] = form.astype(BF16)
 
     lane = lax.broadcasted_iota(jnp.int32, (1, own), 1) // BLK
-
-    def columns(peer):
-        forms = [col_stack(form) for form in receiver_forms(col_geom[peer])]
+    group = tile.shape[1] // own
+
+    def columns(peer, first):
+        forms = receiver_forms(col_geom[peer])
         spaced = jnp.concatenate([jnp.where(lane == b, forms[0], 0.0) for b in range(blocks)], axis=0)
-        side_a = spaced.T.astype(BF16)
-        side_b = forms[1].T.astype(BF16)
-        side_s = forms[2].T.astype(BF16)
+        side_a = spaced.astype(BF16).T
+        side_b = forms[1].astype(BF16).T
+        side_s = forms[2].astype(BF16).T
         weight = col_wt[peer]
 
-        def rows(number, total):
-            start = pl.multiple_of(number * own, own)
-            base = form_a[number]
-            masked = jnp.concatenate(
-                [
-                    base * mask[pl.ds(peer * blocks + b, 1), pl.ds(start, own)].astype(BF16)
-                    for b in range(blocks)
-                ],
-                axis=0,
-            )
-            cos_emit = jnp.maximum(dot(side_a, masked, 1, 0), 0.0)
-            cos_recv = jnp.maximum(dot(side_b, form_b[number], 1, 0), 0.0)
-            spread = dot(side_s, form_s[number], 1, 0)
-            tile = (cos_emit * cos_recv * pl.reciprocal(spread * spread, approx=True)).astype(BF16)
-            adj_part[number] += dot(weight, tile, 1, 0)
-            return total + dot(row_val[number], tile, 1, 1)
-
-        zero = jnp.zeros(fwd_part.shape[1:], F32)
-        fwd_part[peer] = lax.fori_loop(0, recv_count, rows, zero, unroll=recv_count <= 4)
+        def rows(chunk, total):
+            for inner in range(group):
+                number = chunk * group + inner
+                start = pl.multiple_of(number * own, own)
+                base = form_a[number]
+                masked = jnp.concatenate(
+                    [
+                        base * mask[pl.ds(peer * blocks + b, 1), pl.ds(start, own)].astype(BF16)
+                        for b in range(blocks)
+                    ],
+                    axis=0,
+                )
+                cos_emit = jnp.maximum(dot(side_a, masked, 1, 0), 0.0)
+                cos_recv = jnp.maximum(dot(side_b, form_b[number], 1, 0), 0.0)
+                spread = dot(side_s, form_s[number], 1, 0)
+                tile[:, inner * own : (inner + 1) * own] = (
+                    cos_emit * cos_recv * pl.reciprocal(spread * spread, approx=True)
+                ).astype(BF16)
+            whole = tile[...]
+            back = dot(weight, whole, 1, 0)
+            for inner in range(group):
+                number = chunk * group + inner
+                piece = back[:, inner * own : (inner + 1) * own]
+                adj_part[number] = piece if first else adj_part[number] + piece
+            width = group * own
+            value = value_t[pl.ds(pl.multiple_of(chunk * width, width), width), :]
+            return total + dot(whole, value, 1, 0)
+
+        total = jnp.zeros((own, value_t.shape[1]), F32)
+        if recv_count == group:
+            total = rows(0, total)
+        else:
+            total = lax.fori_loop(0, recv_count // group, rows, total)
+        fwd_part[peer] = total.T
 
     for k in range(1, recv_count):
         arrival(row_val, val_send, val_recv, "recv", partner(r, k, recv_count)).wait_recv()
+    for k in range(recv_count):
+        value_t[k * own : (k + 1) * own, :] = row_val[k].T
 
     fwd_out = copies(fwd_part, fwd_got, fwd_send, fwd_recv, "emit", e, emit_count, False)
-    columns(e)
+    columns(e, True)
     for k in reversed(range(1, emit_count)):
         peer = partner(e, k, emit_count)
         arrival(col_geom, geom_col_send, geom_col_recv, "emit", peer).wait_recv()
         arrival(col_wt, wt_send, wt_recv, "emit", peer).wait_recv()
-        columns(peer)
+        columns(peer, False)
         fwd_out[k - 1].start()
 
     ret_out = copies(adj_part, adj_got, ret_send, ret_recv, "recv", r, recv_count, False)
@@ -301,14 +340,16 @@
     low = (weights - high.astype(F32)).astype(BF16)
     source = dot(high, selector, 1, 1) + dot(low, selector, 1, 1)
 
+    share = emis_ref[...]
+    emission = emission_ref[...]
+
     incoming = fwd_part[e]
     for k in range(1, emit_count):
         peer = partner(e, k, emit_count)
         arrival(fwd_got, fwd_send, fwd_recv, "emit", peer).wait_recv()
         incoming = incoming + fwd_got[peer]
-    emission = emission_ref[...]
-    share = emis_ref[...]
     out_rad[...] = share * emission + (1.0 - share) * incoming
+    stores[0].start()
     returned = adj_part[r]
     for k in range(1, recv_count):
         peer = partner(r, k, recv_count)
@@ -316,10 +357,14 @@
         returned = returned + adj_got[peer]
     adjoint = source + returned
     out_adj[...] = adjoint
+    stores[1].start()
     out_grad[...] = jnp.sum(adjoint * (emission - incoming), axis=0, keepdims=True)
+    stores[2].start()
 
     for copy in row_geom_out + col_geom_out + val_out + wt_out + fwd_out + ret_out:
         copy.wait_send()
+    for copy in stores:
+        copy.wait()
 
 
 def finish(rad_ref, adj_ref, grad_ref, rad_hbm, adj_hbm, grad_hbm, sem):
@@ -352,7 +397,7 @@
     cases = emission.shape[0]
     blocks = own // BLK
     row_total = own * recv_count
-    vmem = pl.BlockSpec(memory_space=pltpu.VMEM)
+    group = math.gcd(recv_count, 4)
     hbm = pl.BlockSpec(memory_space=pltpu.HBM)
     emit_sem = pltpu.SemaphoreType.DMA((emit_count,))
     recv_sem = pltpu.SemaphoreType.DMA((recv_count,))
@@ -374,10 +419,12 @@
         functools.partial(sweep, emit_count, recv_count),
         out_shape=results,
         in_specs=[hbm] * len(operands),
-        out_specs=(vmem, vmem, vmem),
+        out_specs=(hbm,) * 3,
         scratch_shapes=[pltpu.VMEM(x.shape, x.dtype) for x in operands]
+        + [pltpu.VMEM(x.shape, x.dtype) for x in results]
         + [
             pltpu.SemaphoreType.DMA((len(operands),)),
+            pltpu.SemaphoreType.DMA((3,)),
             pltpu.VMEM((recv_count, 8, own), F32),
             pltpu.VMEM((emit_count, 8, own), F32),
             pltpu.VMEM((recv_count, cases, own), BF16),
@@ -386,6 +433,8 @@
             pltpu.VMEM((recv_count, 48, own), BF16),
             pltpu.VMEM((recv_count, 48, own), BF16),
             pltpu.VMEM((recv_count, 48, own), BF16),
+            pltpu.VMEM((own, own * group), BF16),
+            pltpu.VMEM((row_total, cases), BF16),
             pltpu.VMEM((emit_count, cases, own), F32),
             pltpu.VMEM((emit_count, cases, own), F32),
             pltpu.VMEM((recv_count, cases, own), F32),
@@ -404,16 +453,17 @@
             recv_sem,
         ],
         compiler_params=pltpu.CompilerParams(
-            collective_id=0, has_side_effects=True, vmem_limit_bytes=40 * 1024 * 1024
+            collective_id=0, has_side_effects=True, vmem_limit_bytes=64 * 1024 * 1024
         ),
         name="sweep",
     )(*operands)
     radiosity_out, adjoint_out, grad = pl.pallas_call(
         finish,
         out_shape=results,
-        in_specs=[vmem, vmem, vmem],
-        out_specs=(hbm, hbm, hbm),
+        in_specs=[hbm] * 3,
+        out_specs=(hbm,) * 3,
         scratch_shapes=[pltpu.SemaphoreType.DMA((3,))],
+        compiler_params=pltpu.CompilerParams(vmem_limit_bytes=64 * 1024 * 1024),
         name="finish",
     )(*swept)
     return (radiosity_out, adjoint_out, grad[0])

time: 28.6 us -> 20.8 us (0.73); the launches traced: 28 us -> 20.7 us
  local copies, waits for them, and re-layouts: 8.44 us -> 0 us
  Pallas kernels: 18.9 us -> 20 us
    unnamed x26 -> x0, local copies, waits for them, and re-layouts: 8.44 us -> none
    pallas_call x1, Pallas kernels: 1.43 us -> 3.15 us  [local(): pl.pallas_call(finish, out_shape=results, in_specs=[hbm] * 3, out_specs=(...]
    pallas_call x1, Pallas kernels: 17.5 us -> 16.9 us  [local(): pl.pallas_call(functools.partial(sweep, emit_count, recv_count), out_shap...]
where the time goes in v4:
time: 20.8 us; the launch traced here: 20.7 us
  Pallas kernels  20 us (96%)
  between operations  0.64 us (3%)
    pallas_call x1, Pallas kernels, local(): pl.pallas_call(functools.partial(sweep, emit_count, recv_count), out_shap...  16.9 us
    pallas_call x1, Pallas kernels, local(): pl.pallas_call(finish, out_shape=results, in_specs=[hbm] * 3, out_specs=(...  3.15 us

profile of v4, /device:TPU:0, one launch (start us, length us, event | category | flops | bytes accessed | tf_op | source)
XLA Modules:
  0.0 20.7 jit_solution(5503440707124844425)
XLA Ops:
  0.6 16.9 %sweep.1 = (f32[32,256]{1,0:T(8,128)}, f32[32,256]{1,0:T(8,128)}, f32[1,256]{1,0:T(1,128)}) custom-call(f32[3,256]{1,0:T(4,128)} %pos_hbm.1, f32[2,256]{1,0:T(2,128)} %ang_hbm.1, f32[1,256]{1,0:T(1,128)} %bitcast.5, f32[1,256]{1,0:T(1,128)} %bitcast.6, f32[32,256]{1,0:T(8,128)} %rad_hbm.1, f32[32,256]{1,0:T(8,128)} %adj_hbm.1, s32[8,32]{1,0:T(8,128)} %vis_hbm.1, ...), custom_call_target="tpu_custom_call" | custom-call | tf_op jit(solution)/shard_map/sweep/pallas_call | solution.py:418
  17.5 3.1 %finish.1 = (f32[32,256]{1,0:T(8,128)}, f32[32,256]{1,0:T(8,128)}, f32[1,256]{1,0:T(1,128)}) custom-call(f32[32,256]{1,0:T(8,128)} %get-tuple-element.9.rad_ref, f32[32,256]{1,0:T(8,128)} %get-tuple-element.10.adj_ref, f32[1,256]{1,0:T(1,128)} %get-tuple-element.11.grad_ref), custom_call_target="tpu_custom_call" | custom-call | tf_op jit(solution)/shard_map/finish/pallas_call | solution.py:460

commit v5 on v4

--- a/solution.py
+++ b/solution.py
@@ -270,33 +270,42 @@
     lane = lax.broadcasted_iota(jnp.int32, (1, own), 1) // BLK
     group = tile.shape[1] // own
 
-    def columns(peer, first):
-        forms = receiver_forms(col_geom[peer])
-        spaced = jnp.concatenate([jnp.where(lane == b, forms[0], 0.0) for b in range(blocks)], axis=0)
-        side_a = spaced.astype(BF16).T
-        side_b = forms[1].astype(BF16).T
-        side_s = forms[2].astype(BF16).T
-        weight = col_wt[peer]
+    def columns(peers, first):
+        side_a, side_b, side_s = [], [], []
+        for peer in peers:
+            forms = receiver_forms(col_geom[peer])
+            spaced = jnp.concatenate(
+                [jnp.where(lane == b, forms[0], 0.0) for b in range(blocks)], axis=0
+            )
+            side_a.append(spaced.astype(BF16).T)
+            side_b.append(forms[1].astype(BF16).T)
+            side_s.append(forms[2].astype(BF16).T)
+        side_b = jnp.concatenate(side_b, axis=0)
+        side_s = jnp.concatenate(side_s, axis=0)
+        weight = jnp.concatenate([col_wt[peer] for peer in peers], axis=1)
+        height = own * len(peers)
 
         def rows(chunk, total):
             for inner in range(group):
                 number = chunk * group + inner
                 start = pl.multiple_of(number * own, own)
                 base = form_a[number]
-                masked = jnp.concatenate(
-                    [
-                        base * mask[pl.ds(peer * blocks + b, 1), pl.ds(start, own)].astype(BF16)
-                        for b in range(blocks)
-                    ],
-                    axis=0,
-                )
-                cos_emit = jnp.maximum(dot(side_a, masked, 1, 0), 0.0)
+                across = slice(inner * own, (inner + 1) * own)
                 cos_recv = jnp.maximum(dot(side_b, form_b[number], 1, 0), 0.0)
                 spread = dot(side_s, form_s[number], 1, 0)
-                tile[:, inner * own : (inner + 1) * own] = (
-                    cos_emit * cos_recv * pl.reciprocal(spread * spread, approx=True)
-                ).astype(BF16)
-            whole = tile[...]
+                ratio = cos_recv * pl.reciprocal(spread * spread, approx=True)
+                for n, peer in enumerate(peers):
+                    masked = jnp.concatenate(
+                        [
+                            base * mask[pl.ds(peer * blocks + b, 1), pl.ds(start, own)].astype(BF16)
+                            for b in range(blocks)
+                        ],
+                        axis=0,
+                    )
+                    cos_emit = jnp.maximum(dot(side_a[n], masked, 1, 0), 0.0)
+                    down = slice(n * own, (n + 1) * own)
+                    tile[down, across] = (cos_emit * ratio[down]).astype(BF16)
+            whole = tile[:height, :]
             back = dot(weight, whole, 1, 0)
             for inner in range(group):
                 number = chunk * group + inner
@@ -306,12 +315,13 @@
             value = value_t[pl.ds(pl.multiple_of(chunk * width, width), width), :]
             return total + dot(whole, value, 1, 0)
 
-        total = jnp.zeros((own, value_t.shape[1]), F32)
+        total = jnp.zeros((height, value_t.shape[1]), F32)
         if recv_count == group:
             total = rows(0, total)
         else:
             total = lax.fori_loop(0, recv_count // group, rows, total)
-        fwd_part[peer] = total.T
+        for n, peer in enumerate(peers):
+            fwd_part[peer] = total[n * own : (n + 1) * own].T
 
     for k in range(1, recv_count):
         arrival(row_val, val_send, val_recv, "recv", partner(r, k, recv_count)).wait_recv()
@@ -319,13 +329,17 @@
         value_t[k * own : (k + 1) * own, :] = row_val[k].T
 
     fwd_out = copies(fwd_part, fwd_got, fwd_send, fwd_recv, "emit", e, emit_count, False)
-    columns(e, True)
-    for k in reversed(range(1, emit_count)):
-        peer = partner(e, k, emit_count)
-        arrival(col_geom, geom_col_send, geom_col_recv, "emit", peer).wait_recv()
-        arrival(col_wt, wt_send, wt_recv, "emit", peer).wait_recv()
-        columns(peer, False)
-        fwd_out[k - 1].start()
+    together = tile.shape[0] // own
+    for low in range(1, emit_count, together):
+        numbers = range(low, min(low + together, emit_count))
+        peers = [partner(e, k, emit_count) for k in numbers]
+        for peer in peers:
+            arrival(col_geom, geom_col_send, geom_col_recv, "emit", peer).wait_recv()
+            arrival(col_wt, wt_send, wt_recv, "emit", peer).wait_recv()
+        columns(peers, low == 1)
+        for k in numbers:
+            fwd_out[k - 1].start()
+    columns([e], emit_count == 1)
 
     ret_out = copies(adj_part, adj_got, ret_send, ret_recv, "recv", r, recv_count, False)
     for copy in ret_out:
@@ -367,16 +381,20 @@
         copy.wait()
 
 
-def finish(rad_ref, adj_ref, grad_ref, rad_hbm, adj_hbm, grad_hbm, sem):
-    stores = [
-        pltpu.make_async_copy(rad_ref, rad_hbm, sem.at[0]),
-        pltpu.make_async_copy(adj_ref, adj_hbm, sem.at[1]),
-        pltpu.make_async_copy(grad_ref, grad_hbm, sem.at[2]),
-    ]
-    for copy in stores:
-        copy.start()
-    for copy in stores:
-        copy.wait()
+def finish(rad_in, adj_in, grad_in, rad_out, adj_out, grad_out, rad, adj, grad, load_sem, store_sem):
+    loads, stores = [], []
+    for n, (src, held, dst) in enumerate(
+        ((rad_in, rad, rad_out), (adj_in, adj, adj_out), (grad_in, grad, grad_out))
+    ):
+        loads.append(pltpu.make_async_copy(src, held, load_sem.at[n]))
+        stores.append(pltpu.make_async_copy(held, dst, store_sem.at[n]))
+    for load in loads:
+        load.start()
+    for load, store in zip(loads, stores):
+        load.wait()
+        store.start()
+    for store in stores:
+        store.wait()
 
 
 def local(
@@ -433,7 +451,7 @@
             pltpu.VMEM((recv_count, 48, own), BF16),
             pltpu.VMEM((recv_count, 48, own), BF16),
             pltpu.VMEM((recv_count, 48, own), BF16),
-            pltpu.VMEM((own, own * group), BF16),
+            pltpu.VMEM((own * max(1, min(3, emit_count - 1)), own * group), BF16),
             pltpu.VMEM((row_total, cases), BF16),
             pltpu.VMEM((emit_count, cases, own), F32),
             pltpu.VMEM((emit_count, cases, own), F32),
@@ -462,7 +480,8 @@
         out_shape=results,
         in_specs=[hbm] * 3,
         out_specs=(hbm,) * 3,
-        scratch_shapes=[pltpu.SemaphoreType.DMA((3,))],
+        scratch_shapes=[pltpu.VMEM(x.shape, x.dtype) for x in results]
+        + [pltpu.SemaphoreType.DMA((3,)), pltpu.SemaphoreType.DMA((3,))],
         compiler_params=pltpu.CompilerParams(vmem_limit_bytes=64 * 1024 * 1024),
         name="finish",
     )(*swept)

time: 20.8 us -> 20.3 us (0.976)
  Pallas kernels: 20 us -> 19.5 us
    pallas_call x1, Pallas kernels: 3.15 us -> 1.44 us  [local(): pl.pallas_call(finish, out_shape=results, in_specs=[hbm] * 3, out_specs=(...]
    pallas_call x1, Pallas kernels: 16.9 us -> 18.1 us  [local(): pl.pallas_call(functools.partial(sweep, emit_count, recv_count), out_shap...]
where the time goes in v5:
time: 20.3 us; the launch traced here: 20.1 us
  Pallas kernels  19.5 us (96%)
  between operations  0.64 us (3%)
    pallas_call x1, Pallas kernels, local(): pl.pallas_call(functools.partial(sweep, emit_count, recv_count), out_shap...  18.1 us
    pallas_call x1, Pallas kernels, local(): pl.pallas_call(finish, out_shape=results, in_specs=[hbm] * 3, out_specs=(...  1.44 us

profile of v5, /device:TPU:0, one launch (start us, length us, event | category | flops | bytes accessed | tf_op | source)
XLA Modules:
  0.0 20.1 jit_solution(3784339802481518630)
XLA Ops:
  0.6 18.1 %sweep.1 = (f32[32,256]{1,0:T(8,128)}, f32[32,256]{1,0:T(8,128)}, f32[1,256]{1,0:T(1,128)}) custom-call(f32[3,256]{1,0:T(4,128)} %pos_hbm.1, f32[2,256]{1,0:T(2,128)} %ang_hbm.1, f32[1,256]{1,0:T(1,128)} %bitcast.5, f32[1,256]{1,0:T(1,128)} %bitcast.6, f32[32,256]{1,0:T(8,128)} %rad_hbm.1, f32[32,256]{1,0:T(8,128)} %adj_hbm.1, s32[8,32]{1,0:T(8,128)} %vis_hbm.1, ...), custom_call_target="tpu_custom_call" | custom-call | tf_op jit(solution)/shard_map/sweep/pallas_call | solution.py:436
  18.7 1.4 %finish.1 = (f32[32,256]{1,0:T(8,128)}, f32[32,256]{1,0:T(8,128)}, f32[1,256]{1,0:T(1,128)}) custom-call(f32[32,256]{1,0:T(8,128)} %get-tuple-element.9.rad_in, f32[32,256]{1,0:T(8,128)} %get-tuple-element.10.adj_in, f32[1,256]{1,0:T(1,128)} %get-tuple-element.11.grad_in), custom_call_target="tpu_custom_call" | custom-call | tf_op jit(solution)/shard_map/finish/pallas_call | solution.py:478

commit v6 on v4

--- a/solution.py
+++ b/solution.py
@@ -270,7 +270,7 @@
     lane = lax.broadcasted_iota(jnp.int32, (1, own), 1) // BLK
     group = tile.shape[1] // own
 
-    def columns(peer, first):
+    def columns(peer, first, last):
         forms = receiver_forms(col_geom[peer])
         spaced = jnp.concatenate([jnp.where(lane == b, forms[0], 0.0) for b in range(blocks)], axis=0)
         side_a = spaced.astype(BF16).T
@@ -302,6 +302,9 @@
                 number = chunk * group + inner
                 piece = back[:, inner * own : (inner + 1) * own]
                 adj_part[number] = piece if first else adj_part[number] + piece
+            if last and recv_count == group:
+                for copy in ret_out:
+                    copy.start()
             width = group * own
             value = value_t[pl.ds(pl.multiple_of(chunk * width, width), width), :]
             return total + dot(whole, value, 1, 0)
@@ -312,24 +315,25 @@
         else:
             total = lax.fori_loop(0, recv_count // group, rows, total)
         fwd_part[peer] = total.T
+        if last and recv_count != group:
+            for copy in ret_out:
+                copy.start()
 
     for k in range(1, recv_count):
         arrival(row_val, val_send, val_recv, "recv", partner(r, k, recv_count)).wait_recv()
     for k in range(recv_count):
         value_t[k * own : (k + 1) * own, :] = row_val[k].T
 
+    ret_out = copies(adj_part, adj_got, ret_send, ret_recv, "recv", r, recv_count, False)
     fwd_out = copies(fwd_part, fwd_got, fwd_send, fwd_recv, "emit", e, emit_count, False)
-    columns(e, True)
+    columns(e, True, emit_count == 1)
     for k in reversed(range(1, emit_count)):
         peer = partner(e, k, emit_count)
         arrival(col_geom, geom_col_send, geom_col_recv, "emit", peer).wait_recv()
         arrival(col_wt, wt_send, wt_recv, "emit", peer).wait_recv()
-        columns(peer, False)
+        columns(peer, False, k == 1)
         fwd_out[k - 1].start()
 
-    ret_out = copies(adj_part, adj_got, ret_send, ret_recv, "recv", r, recv_count, False)
-    for copy in ret_out:
-        copy.start()
 
     for load in loads[7:]:
         load.wait()
@@ -367,16 +371,20 @@
         copy.wait()
 
 
-def finish(rad_ref, adj_ref, grad_ref, rad_hbm, adj_hbm, grad_hbm, sem):
-    stores = [
-        pltpu.make_async_copy(rad_ref, rad_hbm, sem.at[0]),
-        pltpu.make_async_copy(adj_ref, adj_hbm, sem.at[1]),
-        pltpu.make_async_copy(grad_ref, grad_hbm, sem.at[2]),
-    ]
-    for copy in stores:
-        copy.start()
-    for copy in stores:
-        copy.wait()
+def finish(rad_in, adj_in, grad_in, rad_out, adj_out, grad_out, rad, adj, grad, load_sem, store_sem):
+    loads, stores = [], []
+    for n, (src, held, dst) in enumerate(
+        ((rad_in, rad, rad_out), (adj_in, adj, adj_out), (grad_in, grad, grad_out))
+    ):
+        loads.append(pltpu.make_async_copy(src, held, load_sem.at[n]))
+        stores.append(pltpu.make_async_copy(held, dst, store_sem.at[n]))
+    for load in loads:
+        load.start()
+    for load, store in zip(loads, stores):
+        load.wait()
+        store.start()
+    for store in stores:
+        store.wait()
 
 
 def local(
@@ -462,7 +470,8 @@
         out_shape=results,
         in_specs=[hbm] * 3,
         out_specs=(hbm,) * 3,
-        scratch_shapes=[pltpu.SemaphoreType.DMA((3,))],
+        scratch_shapes=[pltpu.VMEM(x.shape, x.dtype) for x in results]
+        + [pltpu.SemaphoreType.DMA((3,)), pltpu.SemaphoreType.DMA((3,))],
         compiler_params=pltpu.CompilerParams(vmem_limit_bytes=64 * 1024 * 1024),
         name="finish",
     )(*swept)

time: 20.8 us -> 19.2 us (0.923)
  Pallas kernels: 20 us -> 18.3 us
    pallas_call x1, Pallas kernels: 3.15 us -> 1.44 us  [local(): pl.pallas_call(finish, out_shape=results, in_specs=[hbm] * 3, out_specs=(...]
where the time goes in v6:
time: 19.2 us; the launch traced here: 19 us
  Pallas kernels  18.3 us (95%)
  between operations  0.64 us (3%)
    pallas_call x1, Pallas kernels, local(): pl.pallas_call(functools.partial(sweep, emit_count, recv_count), out_shap...  16.9 us
    pallas_call x1, Pallas kernels, local(): pl.pallas_call(finish, out_shape=results, in_specs=[hbm] * 3, out_specs=(...  1.44 us

profile of v6, /device:TPU:0, one launch (start us, length us, event | category | flops | bytes accessed | tf_op | source)
XLA Modules:
  0.0 19.0 jit_solution(1691206313208369420)
XLA Ops:
  0.6 16.9 %sweep.1 = (f32[32,256]{1,0:T(8,128)}, f32[32,256]{1,0:T(8,128)}, f32[1,256]{1,0:T(1,128)}) custom-call(f32[3,256]{1,0:T(4,128)} %pos_hbm.1, f32[2,256]{1,0:T(2,128)} %ang_hbm.1, f32[1,256]{1,0:T(1,128)} %bitcast.5, f32[1,256]{1,0:T(1,128)} %bitcast.6, f32[32,256]{1,0:T(8,128)} %rad_hbm.1, f32[32,256]{1,0:T(8,128)} %adj_hbm.1, s32[8,32]{1,0:T(8,128)} %vis_hbm.1, ...), custom_call_target="tpu_custom_call" | custom-call | tf_op jit(solution)/shard_map/sweep/pallas_call | solution.py:426
  17.5 1.4 %finish.1 = (f32[32,256]{1,0:T(8,128)}, f32[32,256]{1,0:T(8,128)}, f32[1,256]{1,0:T(1,128)}) custom-call(f32[32,256]{1,0:T(8,128)} %get-tuple-element.9.rad_in, f32[32,256]{1,0:T(8,128)} %get-tuple-element.10.adj_in, f32[1,256]{1,0:T(1,128)} %get-tuple-element.11.grad_in), custom_call_target="tpu_custom_call" | custom-call | tf_op jit(solution)/shard_map/finish/pallas_call | solution.py:468

commit v7 on v6

--- a/solution.py
+++ b/solution.py
@@ -237,7 +237,7 @@
 
     row_geom_out = copies(row_geom, row_geom, geom_row_send, geom_row_recv, "recv", r, recv_count, True)
     col_geom_out = copies(col_geom, col_geom, geom_col_send, geom_col_recv, "emit", e, emit_count, True)
-    for copy in col_geom_out + row_geom_out:
+    for copy in row_geom_out + col_geom_out[::-1]:
         copy.start()
     for load in loads[3:6]:
         load.wait()
@@ -245,7 +245,7 @@
     col_wt[e] = ((1.0 - emis_ref[...]) * adj_ref[...]).astype(BF16)
     val_out = copies(row_val, row_val, val_send, val_recv, "recv", r, recv_count, True)
     wt_out = copies(col_wt, col_wt, wt_send, wt_recv, "emit", e, emit_count, True)
-    for copy in wt_out + val_out:
+    for copy in val_out + wt_out[::-1]:
         copy.start()
 
     loads[6].wait()
@@ -269,6 +269,15 @@
 
     lane = lax.broadcasted_iota(jnp.int32, (1, own), 1) // BLK
     group = tile.shape[1] // own
+
+    def values_ready():
+        for k in range(1, recv_count):
+            arrival(row_val, val_send, val_recv, "recv", partner(r, k, recv_count)).wait_recv()
+        for k in range(recv_count):
+            value_t[k * own : (k + 1) * own, :] = row_val[k].T
+
+    if recv_count != group:
+        values_ready()
 
     def columns(peer, first, last):
         forms = receiver_forms(col_geom[peer])
@@ -296,6 +305,8 @@
                 tile[:, inner * own : (inner + 1) * own] = (
                     cos_emit * cos_recv * pl.reciprocal(spread * spread, approx=True)
                 ).astype(BF16)
+            if first and recv_count == group:
+                values_ready()
             whole = tile[...]
             back = dot(weight, whole, 1, 0)
             for inner in range(group):
@@ -319,10 +330,6 @@
             for copy in ret_out:
                 copy.start()
 
-    for k in range(1, recv_count):
-        arrival(row_val, val_send, val_recv, "recv", partner(r, k, recv_count)).wait_recv()
-    for k in range(recv_count):
-        value_t[k * own : (k + 1) * own, :] = row_val[k].T
 
     ret_out = copies(adj_part, adj_got, ret_send, ret_recv, "recv", r, recv_count, False)
     fwd_out = copies(fwd_part, fwd_got, fwd_send, fwd_recv, "emit", e, emit_count, False)

time: 19.2 us -> 18.8 us (0.979)
  Pallas kernels: 18.3 us -> 18 us
    pallas_call x1, Pallas kernels: 16.9 us -> 16.5 us  [local(): pl.pallas_call(functools.partial(sweep, emit_count, recv_count), out_shap...]
where the time goes in v7:
time: 18.8 us; the launch traced here: 18.6 us
  Pallas kernels  18 us (96%)
  between operations  0.64 us (3%)
    pallas_call x1, Pallas kernels, local(): pl.pallas_call(functools.partial(sweep, emit_count, recv_count), out_shap...  16.5 us
    pallas_call x1, Pallas kernels, local(): pl.pallas_call(finish, out_shape=results, in_specs=[hbm] * 3, out_specs=(...  1.44 us

profile of v7, /device:TPU:0, one launch (start us, length us, event | category | flops | bytes accessed | tf_op | source)
XLA Modules:
  0.0 18.6 jit_solution(15325977679742134568)
XLA Ops:
  0.6 16.5 %sweep.1 = (f32[32,256]{1,0:T(8,128)}, f32[32,256]{1,0:T(8,128)}, f32[1,256]{1,0:T(1,128)}) custom-call(f32[3,256]{1,0:T(4,128)} %pos_hbm.1, f32[2,256]{1,0:T(2,128)} %ang_hbm.1, f32[1,256]{1,0:T(1,128)} %bitcast.5, f32[1,256]{1,0:T(1,128)} %bitcast.6, f32[32,256]{1,0:T(8,128)} %rad_hbm.1, f32[32,256]{1,0:T(8,128)} %adj_hbm.1, s32[8,32]{1,0:T(8,128)} %vis_hbm.1, ...), custom_call_target="tpu_custom_call" | custom-call | tf_op jit(solution)/shard_map/sweep/pallas_call | solution.py:433
  17.2 1.4 %finish.1 = (f32[32,256]{1,0:T(8,128)}, f32[32,256]{1,0:T(8,128)}, f32[1,256]{1,0:T(1,128)}) custom-call(f32[32,256]{1,0:T(8,128)} %get-tuple-element.9.rad_in, f32[32,256]{1,0:T(8,128)} %get-tuple-element.10.adj_in, f32[1,256]{1,0:T(1,128)} %get-tuple-element.11.grad_in), custom_call_target="tpu_custom_call" | custom-call | tf_op jit(solution)/shard_map/finish/pallas_call | solution.py:475
